TPU v7x, 32 devices: a whole 2x2x4 slice. The times are simulated.
32 devices in a mesh: groups: 2 (over y), ctx: 4 (over z), head: 4 (over x, core).
Axes of the slice: x: 2, y: 2, z: 4, core: 2. Of those that a mesh axis runs over, the one named last changes fastest.
Arguments:
- q_block: bfloat16 [2048, 8192], P(('groups', 'ctx'), 'head'), parts along dimension 0, may hold values from -6 to 6
- kv_block: bfloat16 [2, 2048, 1024], P(None, ('groups', 'ctx'), 'head'), parts along dimension 1, may hold values from -6 to 6
- anchor_kv: bfloat16 [2, 1024, 1024], P(None, ('groups', 'ctx'), 'head'), parts along dimension 1, may hold values from -6 to 6
- cache_kv: bfloat16 [2, 32768, 1024], P(None, ('groups', 'ctx'), 'head'), parts along dimension 1, may hold values from -6 to 6
- cache_len: int32 [8], P(('groups', 'ctx')), parts along dimension 0, may hold values from 1 to 4096, 8192 in all
- query_q: bfloat16 [128, 8192], P(('groups', 'ctx'), 'head'), parts along dimension 0, may hold values from -6 to 6
- query_kv: bfloat16 [2, 128, 1024], P(None, ('groups', 'ctx'), 'head'), parts along dimension 1, may hold values from -6 to 6
- query_pos: int32 [128], P('groups'), parts along dimension 0, may hold values from 0 to 63, each once
Outputs:
- block_out: bfloat16 [2048, 8192], P(('groups', 'ctx'), 'head'), parts along dimension 0
- query_out: bfloat16 [128, 8192], P(('groups', 'ctx'), 'head'), parts along dimension 0
There are 2 independent parts, one for each index of `groups`. A program takes and returns all parts, laid end to end along the dimension named above; each array names one. Nothing has to cross between parts.
All inputs are finite; a program needn't handle non-finite values. No bound on the sum of `cache_len` on one device may be relied on, other than what follows from the above.
Results may differ from a plain program's by a relative error of at most 0.0034.
Values may be sent and summed in bfloat16 or wider, within the bound.
A program may use at most 128 MiB of HBM per device.

v0:
```python
import jax
import jax.numpy as jnp
from jax import lax
from jax.sharding import PartitionSpec as P

HD = 128


masked_score = -1e30


def combined_all(value, axis, join):
    pieces = jax.tree.map(lambda part: lax.all_gather(part, axis), value)
    head = jax.tree.map(lambda part: part[0], pieces)
    tail = jax.tree.map(lambda part: part[1:], pieces)
    subtotal, _ = lax.scan(lambda subtotal, section: (join(subtotal, section), None), head, tail)
    return subtotal


def widen(per_head):
    return jnp.repeat(per_head, HD, axis=-1)


def partial_attention(queries, key_rows, value_rows, visible):
    row_count = queries.shape[0]
    key_count = key_rows.shape[0]
    kv_heads = key_rows.shape[1] // HD
    query_heads = queries.shape[1] // HD
    group_size = query_heads // kv_heads
    grouped = queries.reshape(row_count, kv_heads, group_size, HD)
    key_heads = key_rows.reshape(key_count, kv_heads, HD)
    scores = jnp.einsum(
        "rkgd,skd->rkgs", grouped, key_heads, preferred_element_type=jnp.float32
    ) * (1.0 / jnp.sqrt(jnp.float32(HD)))
    scores = jnp.where(visible[:, None, None, :], scores, masked_score)
    peak_score = jnp.max(scores, axis=-1)
    weights = jnp.exp(scores - peak_score[..., None])
    totals = jnp.sum(weights, axis=-1)
    value_heads = value_rows.reshape(key_count, kv_heads, HD)
    output = jnp.einsum(
        "rkgs,skd->rkgd",
        weights.astype(jnp.bfloat16),
        value_heads,
        preferred_element_type=jnp.float32,
    )
    return (
        peak_score.reshape(row_count, query_heads),
        totals.reshape(row_count, query_heads),
        output.reshape(row_count, query_heads * HD),
    )


def combine_parts(first, second):
    top_score = jnp.maximum(first[0], second[0])
    left_factor = jnp.exp(first[0] - top_score)
    right_factor = jnp.exp(second[0] - top_score)
    return (
        top_score,
        first[1] * left_factor + second[1] * right_factor,
        first[2] * widen(left_factor) + second[2] * widen(right_factor),
    )


def local(q_block, kv_block, anchor_kv, cache_kv, cache_len, query_q, query_kv, query_pos):
    anchor = lax.all_gather(anchor_kv, "ctx", axis=1, tiled=True)
    anchor_count = anchor.shape[1]
    block_count = q_block.shape[0]
    causal = jnp.arange(block_count)[None, :] <= jnp.arange(block_count)[:, None]
    block_visible = jnp.concatenate([jnp.ones((block_count, anchor_count), bool), causal], axis=1)
    block_parts = partial_attention(
        q_block,
        jnp.concatenate([anchor[0], kv_block[0]], axis=0),
        jnp.concatenate([anchor[1], kv_block[1]], axis=0),
        block_visible,
    )
    block_out = (block_parts[2] / widen(block_parts[1])).astype(jnp.bfloat16)
    all_queries, all_query_kv = (
        lax.all_gather(query_q, "ctx", axis=0, tiled=True),
        lax.all_gather(query_kv, "ctx", axis=1, tiled=True),
    )
    query_total = all_queries.shape[0]
    cache_count = cache_kv.shape[1]
    in_cache = jnp.arange(cache_count, dtype=jnp.int32) < cache_len[0]
    context_visible = jnp.concatenate(
        [
            jnp.broadcast_to(in_cache[None, :], (query_total, cache_count)),
            jnp.ones((query_total, block_count), bool),
        ],
        axis=1,
    )
    context_peak, context_totals, context_output = partial_attention(
        all_queries,
        jnp.concatenate([cache_kv[0], kv_block[0]], axis=0),
        jnp.concatenate([cache_kv[1], kv_block[1]], axis=0),
        context_visible,
    )
    own_count = query_q.shape[0]
    first_row = lax.axis_index("ctx") * own_count
    own_positions = lax.dynamic_slice_in_dim(query_pos, first_row, own_count)
    local_visible = jnp.concatenate(
        [jnp.ones((own_count, anchor_count), bool), query_pos[None, :] <= own_positions[:, None]],
        axis=1,
    )
    local_parts = partial_attention(
        query_q,
        jnp.concatenate([anchor[0], all_query_kv[0]], axis=0),
        jnp.concatenate([anchor[1], all_query_kv[1]], axis=0),
        local_visible,
    )
    merged = combined_all((context_peak, context_totals, context_output), "ctx", combine_parts)
    remote = tuple(
        (lax.dynamic_slice_in_dim(merged_part, first_row, own_count, 0) for merged_part in merged)
    )
    final_parts = combine_parts(remote, local_parts)
    query_out = (final_parts[2] / widen(final_parts[1])).astype(jnp.bfloat16)
    return (block_out, query_out)


def solution(mesh):
    in_specs = (
        P(("groups", "ctx"), "head"),
        P(None, ("groups", "ctx"), "head"),
        P(None, ("groups", "ctx"), "head"),
        P(None, ("groups", "ctx"), "head"),
        P(("groups", "ctx")),
        P(("groups", "ctx"), "head"),
        P(None, ("groups", "ctx"), "head"),
        P("groups"),
    )
    out_specs = (P(("groups", "ctx"), "head"), P(("groups", "ctx"), "head"))
    return jax.shard_map(local, mesh=mesh, in_specs=in_specs, out_specs=out_specs, check_vma=False)
```

profile of v0, /device:TPU:0, one launch (start us, length us, event | category | flops | bytes accessed | tf_op | source)
XLA Modules:
  0.0 164.5 jit_solution(15794202108696513625)
XLA Ops:
  7.2 1.0 fusion.62
  8.2 0.1 copy.89
  8.3 0.1 copy.58
  9.1 4.4 %fusion.60 = (bf16[1,4096,256]{2,1,0:T(8,128)(2,1)}, bf16[1,4096,256]{2,1,0:T(8,128)(2,1)}) fusion(bf16[2,4096,256]{2,1,0:T(8,128)(2,1)} %param.13), kind=kLoop, calls=%fused_computation.85 | loop fusion | bytes 8388608 | tf_op jit(solution)/shard_map/slice | solution.py:94
  13.5 2.9 %copy.90 = bf16[1,4096,256]{1,2,0:T(8,128)(2,1)S(1)} copy(bf16[1,4096,256]{2,1,0:T(8,128)(2,1)} %get-tuple-element.66) | data formatting | bytes 4194304
  16.5 2.5 %copy.64 = bf16[4096,2,128]{2,0,1:T(8,128)(2,1)} copy(bf16[4096,2,128]{0,2,1:T(8,128)(2,1)S(1)} %bitcast.172) | data formatting | bytes 4194304 | tf_op jit(solution)/shard_map/concatenate | solution.py:93
  19.0 15.6 %all_gather.19 = bf16[64,2048]{1,0:T(8,128)(2,1)S(1)} all-gather(bf16[16,2048]{1,0:T(8,128)(2,1)S(1)} %copy-done.3), channel_id=1, replica_groups=mesh['groups'=2,'ctx'=4,'head'=4] {'ctx'}, dimensions={0}, use_global_device_ids=true | all-gather | bytes 327680 | tf_op jit(solution)/shard_map/all_gather | solution.py:78
  34.6 0.1 copy.55
  34.8 0.1 copy.69
  34.9 2.9 %copy.91 = bf16[1,4096,256]{1,2,0:T(8,128)(2,1)S(1)} copy(bf16[1,4096,256]{2,1,0:T(8,128)(2,1)} %get-tuple-element.65) | data formatting | bytes 4194304
  37.8 2.5 %copy.68 = bf16[4096,2,128]{2,0,1:T(8,128)(2,1)} copy(bf16[4096,2,128]{0,2,1:T(8,128)(2,1)S(1)} %bitcast.173) | data formatting | bytes 4194304 | tf_op jit(solution)/shard_map/concatenate | solution.py:94
  40.3 9.4 %bitcast_reduce_fusion = (f32[64,2,8]{0,2,1:T(8,128)S(1)}, f32[2,4352,64,8]{1,2,3,0:T(8,128)}) fusion(pred[4352]{0:T(1024)(128)(4,1)S(1)} %concatenate.56, bf16[64,2,8,128]{3,2,1,0:T(8,128)(2,1)S(1)} %bitcast.190, bf16[256,2,128]{2,0,1:T(8,128)(2,1)S(1)} %copy.58, bf16[4096,2,128]{2,0,1:T(8,128)(2,1)} %copy.64), kind=kOutput, calls=%fused_computation.10 | convolution fusion | flops 1158675456 | bytes 20324608 | tf_op jit(solution)/shard_map/rkgd,skd->rkgs/dot_general | solution.py:32
  49.6 7.8 %fusion.23 = f32[64,2,8,128]{3,0,2,1:T(8,128)S(1)} fusion(f32[2,4352,64,8]{1,2,3,0:T(8,128)} %get-tuple-element.78, f32[64,2,8]{0,2,1:T(8,128)S(1)} %get-tuple-element.77, pred[4352]{0:T(1024)(128)(4,1)S(1)} %concatenate.56, bf16[256,2,128]{2,0,1:T(8,128)(2,1)S(1)} %copy.69, bf16[4096,2,128]{2,0,1:T(8,128)(2,1)S(1)} %copy-done.1), kind=kOutput, calls=%fused_computation.36 | convolution fusion | flops 1163132928 | bytes 20586752 | tf_op jit(solution)/shard_map/rkgs,skd->rkgd/dot_general | solution.py:40
  57.5 0.3 copy.70
  57.8 0.9 all_gather_reshape.11
  58.8 10.1 %fusion.5 = f32[64,2,8]{0,2,1:T(8,128)S(1)} fusion(f32[2,4352,64,8]{1,2,3,0:T(8,128)} %get-tuple-element.78, f32[64,2,8]{0,2,1:T(8,128)S(1)} %get-tuple-element.77, pred[4352]{0:T(1024)(128)(4,1)S(1)} %concatenate.56), kind=kLoop, calls=%fused_computation.14 | loop fusion | flops 17824768 | bytes 17838336 | tf_op jit(solution)/shard_map/reduce_sum | solution.py:38
  68.9 13.6 %all_gather.21 = f32[4,64,16]{1,2,0:T(8,128)S(1)} all-gather(f32[1,64,16]{1,2,0:T(8,128)S(1)} %bitcast.194), channel_id=1, replica_groups=mesh['groups'=2,'ctx'=4,'head'=4] {'ctx'}, dimensions={0}, use_global_device_ids=true | all-gather | bytes 20480 | tf_op jit(solution)/shard_map/all_gather | solution.py:13
  82.5 13.2 %all_gather.20 = f32[4,64,16]{1,2,0:T(8,128)S(1)} all-gather(f32[1,64,16]{1,2,0:T(8,128)S(1)} %bitcast.193), channel_id=1, replica_groups=mesh['groups'=2,'ctx'=4,'head'=4] {'ctx'}, dimensions={0}, use_global_device_ids=true | all-gather | bytes 20480 | tf_op jit(solution)/shard_map/all_gather | solution.py:13
  95.9 0.1 copy.54
  96.0 20.8 %all_gather.18 = bf16[2,512,256]{1,2,0:T(8,128)(2,1)S(1)} all-gather(bf16[2,128,256]{1,2,0:T(8,128)(2,1)S(1)} %copy.54), channel_id=1, replica_groups=mesh['groups'=2,'ctx'=4,'head'=4] {'ctx'}, dimensions={1}, use_global_device_ids=true | all-gather | bytes 655360 | tf_op jit(solution)/shard_map/all_gather | solution.py:65
  116.9 0.2 copy.57
  117.1 13.3 %all_gather.23 = bf16[2,64,256]{2,1,0:T(8,128)(2,1)S(1)} all-gather(bf16[2,16,256]{2,1,0:T(8,128)(2,1)S(1)} %copy-done.7), channel_id=1, replica_groups=mesh['groups'=2,'ctx'=4,'head'=4] {'ctx'}, dimensions={1}, use_global_device_ids=true | all-gather | bytes 81920 | tf_op jit(solution)/shard_map/all_gather | solution.py:79
  130.5 0.1 copy.75
  130.6 0.2 copy.94
  130.9 2.2 %fusion.8 = (f32[256,2,8]{0,2,1:T(8,128)S(1)}, f32[2,768,256,8]{2,1,3,0:T(8,128)S(1)}) fusion(pred[256,768]{0,1:T(8,128)(4,1)S(1)} %concatenate.52, bf16[256,2,8,128]{3,2,1,0:T(8,128)(2,1)S(1)} %bitcast.174, bf16[256,2,128]{2,0,1:T(8,128)(2,1)S(1)} %copy.58, bf16[512,2,128]{2,0,1:T(8,128)(2,1)S(1)} %copy.57), kind=kOutput, calls=%fused_computation.19 | convolution fusion | flops 815525888 | bytes 14237696 | tf_op jit(solution)/shard_map/rkgd,skd->rkgs/dot_general | solution.py:32
  133.1 0.3 fusion.64
  133.4 0.3 convolution_bitcast_fusion
  133.8 4.4 %fusion.12 = f32[2,128,256,8]{2,1,3,0:T(8,128)} fusion(f32[2,768,256,8]{2,1,3,0:T(8,128)S(1)} %get-tuple-element.74, f32[256,2,8]{0,2,1:T(8,128)S(1)} %get-tuple-element.73, pred[256,768]{0,1:T(8,128)(4,1)S(1)} %concatenate.52, bf16[256,2,128]{0,2,1:T(8,128)(2,1)S(1)} %bitcast.186, bf16[512,2,128]{0,2,1:T(8,128)(2,1)S(1)} %bitcast.179), kind=kOutput, calls=%fused_computation.22 | convolution fusion | flops 818675712 | bytes 15286272 | tf_op jit(solution)/shard_map/rkgs,skd->rkgd/dot_general | solution.py:40
  138.2 1.9 %copy.62 = f32[256,2048]{1,0:T(8,128)S(1)} copy(f32[256,2048]{0,1:T(8,128)} %bitcast.175) | data formatting | bytes 4194304 | tf_op jit(solution)/shard_map/reshape | solution.py:49
  140.2 7.2 %fusion.6 = f32[256,2,8]{0,2,1:T(8,128)S(1)} fusion(f32[2,768,256,8]{2,1,3,0:T(8,128)} %copy-done, f32[256,2,8]{0,2,1:T(8,128)S(1)} %get-tuple-element.73, pred[256,768]{0,1:T(8,128)(4,1)S(1)} %concatenate.52), kind=kLoop, calls=%fused_computation.17 | loop fusion | flops 12578816 | bytes 12812288 | tf_op jit(solution)/shard_map/reduce_sum | solution.py:38
  147.3 0.1 copy.61
  147.4 0.2 fusion.28
  147.7 0.6 broadcast_in_dim.73
  148.3 1.8 %fusion.20 = bf16[256,2048]{1,0:T(8,128)(2,1)} fusion(f32[256,2048]{1,0:T(8,128)S(1)} %copy.62, f32[32,8,16,128]{3,2,1,0:T(8,128)S(1)} %bitcast.171), kind=kLoop, calls=%fused_computation.32 | loop fusion | flops 1048576 | bytes 5242880 | tf_op jit(solution)/shard_map/convert_element_type | solution.py:76
  150.1 1.5 slice.67
  151.6 1.1 slice_bitcast_fusion
  152.7 3.5 %while.14 = (s32[]{:T(128)}, f32[64,16]{0,1:T(8,128)S(1)}, f32[64,16]{0,1:T(8,128)S(1)}, f32[64,2048]{1,0:T(8,128)S(1)}, f32[3,64,16]{1,2,0:T(8,128)S(1)}, /*ind...) while((s32[]{:T(128)}, f32[64,16]{0,1:T(8,128)S(1)}, f32[64,16]{0,1:T(8,128)S(1)}, ...), condition=%wide.region_5.6_spmd, body=%wide.region_4.5_spmd.sunk | while | flops 399362 | bytes 3727453 | solution.py:16
  152.9 0.2 broadcast_in_dim.109
  153.1 0.2 broadcast_in_dim.110
  153.3 0.5 fusion.68
  154.0 0.2 broadcast_in_dim.109
  154.3 0.2 broadcast_in_dim.110
  154.5 0.5 fusion.68
  155.2 0.2 broadcast_in_dim.109
  155.4 0.2 broadcast_in_dim.110
  155.7 0.5 fusion.68
  156.5 0.1 broadcast_in_dim.78
  156.8 0.8 fusion.41
  (56 shorter events, 1.6 us)
Async XLA Ops:
  7.2 11.8 %copy-start.3 = (bf16[16,2048]{1,0:T(8,128)(2,1)S(1)}, bf16[16,2048]{1,0:T(8,128)(2,1)}, u32[]{:S(2)}) copy-start(bf16[16,2048]{1,0:T(8,128)(2,1)} %param.15) | copy-start | bytes 196612
  7.2 142.9 %all-gather.2.cloned.1.call-start = ((), (), s32[]{:S(2)}) async-start(), calls=%async_computation | async-start | bytes 2621440 | tf_op jit(solution)/shard_map/all_gather | solution.py:13
  40.3 9.4 %copy-start.1 = (bf16[4096,2,128]{2,0,1:T(8,128)(2,1)S(1)}, bf16[4096,2,128]{2,0,1:T(8,128)(2,1)}, u32[]{:S(2)}) copy-start(bf16[4096,2,128]{2,0,1:T(8,128)(2,1)} %copy.68) | copy-start | bytes 6291460
  58.7 37.0 %copy-start.8 = (s32[64]{0:T(128)S(1)}, s32[64]{0:T(128)}, u32[]{:S(2)}) copy-start(s32[64]{0:T(128)} %param.17) | copy-start | bytes 772
  58.7 37.2 %copy-start.6 = (bf16[2,128,256]{2,1,0:T(8,128)(2,1)S(1)}, bf16[2,128,256]{2,1,0:T(8,128)(2,1)}, u32[]{:S(2)}) copy-start(bf16[2,128,256]{2,1,0:T(8,128)(2,1)} %param.12) | copy-start | bytes 393220
  58.7 58.3 %copy-start.7 = (bf16[2,16,256]{2,1,0:T(8,128)(2,1)S(1)}, bf16[2,16,256]{2,1,0:T(8,128)(2,1)}, u32[]{:S(2)}) copy-start(bf16[2,16,256]{2,1,0:T(8,128)(2,1)} %param.16) | copy-start | bytes 49156
  58.7 71.9 %copy-start.2 = (bf16[256,2048]{1,0:T(8,128)(2,1)S(1)}, bf16[256,2048]{1,0:T(8,128)(2,1)}, u32[]{:S(2)}) copy-start(bf16[256,2048]{1,0:T(8,128)(2,1)} %param.10) | copy-start | bytes 3145732
  82.5 65.2 %copy-start.4 = (f32[4,64,16]{1,2,0:T(8,128)}, f32[4,64,16]{1,2,0:T(8,128)S(1)}, u32[]{:S(2)}) copy-start(f32[4,64,16]{1,2,0:T(8,128)S(1)} %all_gather.21) | copy-start | bytes 49156
  95.7 52.0 %copy-start.5 = (f32[4,64,16]{1,2,0:T(8,128)}, f32[4,64,16]{1,2,0:T(8,128)S(1)}, u32[]{:S(2)}) copy-start(f32[4,64,16]{1,2,0:T(8,128)S(1)} %all_gather.20) | copy-start | bytes 49156
  133.1 5.2 %copy-start = (f32[2,768,256,8]{2,1,3,0:T(8,128)}, f32[2,768,256,8]{2,1,3,0:T(8,128)S(1)}, u32[]{:S(2)}) copy-start(f32[2,768,256,8]{2,1,3,0:T(8,128)S(1)} %get-tuple-element.74) | copy-start | bytes 37748740
  147.7 5.0 %slice-start = ((f32[4,64,16]{1,2,0:T(8,128)}), f32[3,64,16]{1,2,0:T(8,128)S(1)}, s32[]{:S(2)}) async-start(f32[4,64,16]{1,2,0:T(8,128)} %copy-done.4), calls=%async_computation.1 | async-start | bytes 49152 | tf_op jit(solution)/shard_map/slice | solution.py:15
  147.7 5.0 %slice-start.1 = ((f32[4,64,16]{1,2,0:T(8,128)}), f32[3,64,16]{1,2,0:T(8,128)S(1)}, s32[]{:S(2)}) async-start(f32[4,64,16]{1,2,0:T(8,128)} %copy-done.5), calls=%async_computation.2 | async-start | bytes 49152 | tf_op jit(solution)/shard_map/slice | solution.py:15
Sparse Core Ops, SparseCore 0:
  58.8 55.0 all-gather.1
where the time goes:
time: 165 us; the launch traced here: 164 us
  blocking collectives  76.6 us (46%)
  local copies, waits for them, and re-layouts  26.2 us (16%)
  matrix products  24.5 us (15%)
  other arithmetic  21.9 us (13%)
  between operations  15 us (9%)
    all_gather x2, blocking collectives, combined_all(): pieces = jax.tree.map(lambda part: lax.all_gather(part, axis), value)  26.9 us
    all_gather x1, blocking collectives, local(): anchor = lax.all_gather(anchor_kv, 'ctx', axis=1, tiled=True)  20.8 us
    reduce_sum x3, other arithmetic, partial_attention(): totals = jnp.sum(weights, axis=-1)  17.5 us
    all_gather x1, blocking collectives, local(): lax.all_gather(query_q, 'ctx', axis=0, tiled=True)  15.6 us
    all_gather x1, blocking collectives, local(): lax.all_gather(query_kv, 'ctx', axis=1, tiled=True)  13.3 us
    dot_general x3, matrix products, partial_attention(): jnp.einsum('rkgs,skd->rkgd', weights.astype(jnp.bfloat16), value_heads, p...  12.6 us
    dot_general x3, matrix products, partial_attention(): jnp.einsum('rkgd,skd->rkgs', grouped, key_heads, preferred_element_type=j...  11.9 us
    unnamed x25, local copies, waits for them, and re-layouts  6.36 us
  transfers between devices with their start and end apart: 1, of which 0 were waited for; matrix products, arithmetic and copies ran while one was open for 18% of the time, Pallas kernels for 0%

commit v1 on v0

v1 whole, which is shorter than its diff:
```python
import functools
import math

import jax
import jax.numpy as jnp
from jax import lax
from jax.experimental import pallas as pl
from jax.experimental.pallas import tpu as pltpu
from jax.sharding import PartitionSpec as P

HD = 128
NEG = -1e30
SCALE2 = math.log2(math.e) / math.sqrt(HD)
CHUNK = 512
MESH = pl.DeviceIdType.MESH


def scores(queries, keys):
    dims = (((1,), (1,)), ((), ()))
    return lax.dot_general(queries, keys, dims, preferred_element_type=jnp.float32) * SCALE2


def with_ones(values):
    return jnp.concatenate([values, jnp.ones_like(values)], axis=1)


def weighted(weights, values):
    return jnp.dot(weights.astype(jnp.bfloat16), values, preferred_element_type=jnp.float32)


def kernel(
    n, own,
    pos_ref, len_ref, q_hbm, kv_hbm, anchor_hbm, cache_hbm, qq_hbm, qkv_hbm,
    out_ref, qout_ref,
    q_buf, kv_buf, cache_buf, qkv_buf, anchors, queries,
    qg, kx, vx, xbias, s_buf, m_run, acc, kb, vb, causal,
    send_o, send_st, recv_o, recv_st,
    in_sem, q_send, q_recv, a_send, a_recv, o_send, o_recv, st_send, st_recv,
):
    me = lax.axis_index("ctx")
    peers = [lax.rem(me + k, n) for k in range(1, n)]
    rows = qq_hbm.shape[0]
    block = q_buf.shape[0]
    columns = q_buf.shape[1]
    kv_heads = kv_buf.shape[2] // HD
    group = columns // HD // kv_heads
    share = anchor_hbm.shape[1]
    cache_count = cache_buf.shape[1]
    total = n * rows
    extra = kx.shape[1]
    tile = s_buf.shape[0]
    tile_heads = tile // total
    half = group * HD

    loads = [
        pltpu.make_async_copy(qq_hbm, queries.at[pl.ds(pl.multiple_of(me * rows, rows), rows)], in_sem.at[0]),
        pltpu.make_async_copy(anchor_hbm, anchors.at[me], in_sem.at[1]),
        pltpu.make_async_copy(kv_hbm, kv_buf, in_sem.at[2]),
        pltpu.make_async_copy(qkv_hbm, qkv_buf, in_sem.at[3]),
        pltpu.make_async_copy(cache_hbm, cache_buf, in_sem.at[4]),
        pltpu.make_async_copy(q_hbm, q_buf, in_sem.at[5]),
    ]
    for load in loads:
        load.start()

    barrier = pltpu.get_barrier_semaphore()
    for peer in peers:
        pl.semaphore_signal(barrier, inc=1, device_id={"ctx": peer}, device_id_type=MESH)
    pl.semaphore_wait(barrier, n - 1)

    def own_rows(ref, who):
        return ref.at[pl.ds(pl.multiple_of(who * rows, rows), rows)]

    def query_copy(slot, peer):
        return pltpu.make_async_remote_copy(
            src_ref=qq_hbm, dst_ref=own_rows(queries, slot), send_sem=q_send.at[peer],
            recv_sem=q_recv.at[slot], device_id={"ctx": peer}, device_id_type=MESH)

    def anchor_copy(slot, peer):
        return pltpu.make_async_remote_copy(
            src_ref=anchor_hbm, dst_ref=anchors.at[slot], send_sem=a_send.at[peer],
            recv_sem=a_recv.at[slot], device_id={"ctx": peer}, device_id_type=MESH)

    def output_copy(g, slot, peer):
        cols = pl.ds(g * half, half)
        return pltpu.make_async_remote_copy(
            src_ref=send_o.at[pl.ds(pl.multiple_of(peer * rows, rows), rows), cols],
            dst_ref=recv_o.at[slot, :, cols], send_sem=o_send.at[g, peer],
            recv_sem=o_recv.at[g, slot], device_id={"ctx": peer}, device_id_type=MESH)

    def stats_copy(slot, peer):
        return pltpu.make_async_remote_copy(
            src_ref=send_st.at[:, pl.ds(pl.multiple_of(peer * rows, rows), rows)],
            dst_ref=recv_st.at[slot], send_sem=st_send.at[peer],
            recv_sem=st_recv.at[slot], device_id={"ctx": peer}, device_id_type=MESH)

    for peer in peers:
        query_copy(me, peer).start()
    for peer in peers:
        anchor_copy(me, peer).start()

    row = lax.broadcasted_iota(jnp.int32, (total, HD), 0)
    lane = lax.broadcasted_iota(jnp.int32, (total, HD), 1)
    row_pos = jnp.zeros((total, HD), jnp.int32)
    for i in range(n * own):
        row_pos = jnp.where(row == (i // own) * rows + i % own, pos_ref[i], row_pos)
    key_pos = jnp.full((total, HD), 1 << 30, jnp.int32)
    for j in range(own):
        key_pos = jnp.where(lane == j, pos_ref[me * own + j], key_pos)
    xbias[...] = jnp.where(key_pos <= row_pos, 0.0, NEG)
    send_st[...] = jnp.zeros_like(send_st)
    first = lax.broadcasted_iota(jnp.int32, (block, block), 0)
    second = lax.broadcasted_iota(jnp.int32, (block, block), 1)
    causal[...] = jnp.where(second <= first, 0.0, NEG)

    for load in loads:
        load.wait()
    for g in range(kv_heads):
        cols = slice(g * HD, (g + 1) * HD)
        for half_index, target in ((0, kx), (1, vx)):
            target[g, 0:block] = kv_buf[half_index, :, cols]
            target[g, pl.ds(block, share)] = anchors[me, half_index, :, cols]
            target[g, pl.ds(block + share, rows)] = qkv_buf[half_index, :, cols]
            rest = extra - block - share - rows
            if rest:
                target[g, pl.ds(block + share + rows, rest)] = jnp.zeros((rest, HD), jnp.bfloat16)

    for peer in peers:
        query_copy(peer, peer).wait_recv()

    length = len_ref[0]
    chunk_lane = lax.broadcasted_iota(jnp.int32, (1, CHUNK), 1)

    def fold(block_scores):
        parts = [block_scores[:, k:k + HD] for k in range(0, block_scores.shape[1], HD)]
        return functools.reduce(jnp.maximum, parts)

    for g in range(kv_heads):
        cols = slice(g * HD, (g + 1) * HD)

        def one_tile(t, carry):
            for j in range(tile_heads):
                head = g * group + t * tile_heads + j
                qg[j * total:(j + 1) * total] = queries[:, pl.ds(pl.multiple_of(head * HD, HD), HD)]
            near = scores(qg[...], kx[g])
            tail = jnp.concatenate([xbias[...]] * tile_heads, axis=0)
            edge = block + share
            near_parts = [near[:, :edge], near[:, edge:edge + HD] + tail]
            if extra > edge + HD:
                near_parts.append(jnp.full((tile, extra - edge - HD), NEG, jnp.float32))
            near = jnp.concatenate(near_parts, axis=1)
            s_buf[:, cache_count:] = near
            m_run[...] = fold(near)

            def cached_scores(i, carry):
                at = pl.multiple_of(i * CHUNK, CHUNK)
                bias = jnp.where(chunk_lane + at < length, 0.0, NEG)
                part = scores(qg[...], cache_buf[0, pl.ds(at, CHUNK), cols]) + bias
                s_buf[:, pl.ds(at, CHUNK)] = part
                m_run[...] = jnp.maximum(m_run[...], fold(part))
                return carry

            lax.fori_loop(0, cache_count // CHUNK, cached_scores, 0)
            peak = jnp.max(m_run[...], axis=1, keepdims=True)
            m_run[...] = jnp.broadcast_to(peak, m_run.shape)
            weights = jnp.exp2(s_buf[:, cache_count:] - m_run[:, 0:1])
            acc[...] = weighted(weights, with_ones(vx[g]))

            def cached_values(i, carry):
                at = pl.multiple_of(i * CHUNK, CHUNK)
                weights = jnp.exp2(s_buf[:, pl.ds(at, CHUNK)] - m_run[:, 0:1])
                acc[...] += weighted(weights, with_ones(cache_buf[1, pl.ds(at, CHUNK), cols]))
                return carry

            lax.fori_loop(0, cache_count // CHUNK, cached_values, 0)
            for j in range(tile_heads):
                head = g * group + t * tile_heads + j
                span = slice(j * total, (j + 1) * total)
                send_o[:, pl.ds(pl.multiple_of(head * HD, HD), HD)] = acc[span, :HD].astype(jnp.bfloat16)
                send_st[0] = jnp.where(lane == head, m_run[span], send_st[0])
                send_st[1] = jnp.where(lane == head, acc[span, HD:], send_st[1])
            return carry

        if group == tile_heads:
            one_tile(0, 0)
        else:
            lax.fori_loop(0, group // tile_heads, one_tile, 0)
        for peer in peers:
            output_copy(g, me, peer).start()
    for peer in peers:
        stats_copy(me, peer).start()

    for peer in peers:
        anchor_copy(peer, peer).wait_recv()
    for g in range(kv_heads):
        cols = slice(g * HD, (g + 1) * HD)
        for c in range(n):
            kb[g, c * share:(c + 1) * share] = anchors[c, 0, :, cols]
            vb[g, c * share:(c + 1) * share] = with_ones(anchors[c, 1, :, cols])
        kb[g, pl.ds(n * share, block)] = kv_buf[0, :, cols]
        vb[g, pl.ds(n * share, block)] = with_ones(kv_buf[1, :, cols])

        def one_head(j, carry):
            span = pl.ds(pl.multiple_of((g * group + j) * HD, HD), HD)
            part = scores(q_buf[:, span], kb[g])
            part = jnp.concatenate([part[:, :n * share], part[:, n * share:] + causal[...]], axis=1)
            weights = jnp.exp2(part - jnp.max(part, axis=1, keepdims=True))
            result = weighted(weights, vb[g])
            out_ref[:, span] = (result[:, :HD] / result[:, HD:]).astype(jnp.bfloat16)
            return carry

        lax.fori_loop(0, group, one_head, 0, unroll=2)

    for peer in peers:
        stats_copy(peer, peer).wait_recv()
        for g in range(kv_heads):
            output_copy(g, peer, peer).wait_recv()
    mine = pl.ds(pl.multiple_of(me * rows, rows), rows)
    recv_st[me] = send_st[:, mine]
    recv_o[me] = send_o[mine]
    top = functools.reduce(jnp.maximum, [recv_st[c, 0] for c in range(n)])
    factors = [jnp.exp2(recv_st[c, 0] - top) for c in range(n)]
    whole = sum(factors[c] * recv_st[c, 1] for c in range(n))
    heads = columns // HD
    for h in range(heads):
        span = slice(h * HD, (h + 1) * HD)
        merged = sum(
            recv_o[c, :, span].astype(jnp.float32) * factors[c][:, h:h + 1] for c in range(n)
        )
        qout_ref[:, span] = (merged / whole[:, h:h + 1]).astype(jnp.bfloat16)

    for peer in peers:
        query_copy(me, peer).wait_send()
        anchor_copy(me, peer).wait_send()
        stats_copy(me, peer).wait_send()
        for g in range(kv_heads):
            output_copy(g, me, peer).wait_send()


def local(n, q_block, kv_block, anchor_kv, cache_kv, cache_len, query_q, query_kv, query_pos):
    own = query_q.shape[0]
    rows = -(-own // 16) * 16
    if rows != own:
        query_q = jnp.pad(query_q, ((0, rows - own), (0, 0)))
        query_kv = jnp.pad(query_kv, ((0, 0), (0, rows - own), (0, 0)))
    block, columns = q_block.shape
    kv_columns = kv_block.shape[2]
    kv_heads = kv_columns // HD
    group = columns // kv_columns
    share = anchor_kv.shape[1]
    cache_count = cache_kv.shape[1]
    total = n * rows
    tile = total * max(1, min(group, 512 // total))
    extra = -(-(block + share + HD) // HD) * HD
    keys = n * share + block
    bf16, f32 = jnp.bfloat16, jnp.float32
    vmem = pltpu.VMEM
    dma = pltpu.SemaphoreType.DMA
    hbm = pl.BlockSpec(memory_space=pl.ANY)
    smem = pl.BlockSpec(memory_space=pltpu.SMEM)
    block_out, query_out = pl.pallas_call(
        functools.partial(kernel, n, own),
        out_shape=(
            jax.ShapeDtypeStruct((block, columns), bf16),
            jax.ShapeDtypeStruct((rows, columns), bf16),
        ),
        in_specs=[smem, smem] + [hbm] * 6,
        out_specs=(pl.BlockSpec(memory_space=vmem), pl.BlockSpec(memory_space=vmem)),
        scratch_shapes=[
            vmem((block, columns), bf16),
            vmem((2, block, kv_columns), bf16),
            vmem((2, cache_count, kv_columns), bf16),
            vmem((2, rows, kv_columns), bf16),
            vmem((n, 2, share, kv_columns), bf16),
            vmem((total, columns), bf16),
            vmem((tile, HD), bf16),
            vmem((kv_heads, extra, HD), bf16),
            vmem((kv_heads, extra, HD), bf16),
            vmem((total, HD), f32),
            vmem((tile, cache_count + extra), f32),
            vmem((tile, HD), f32),
            vmem((tile, 2 * HD), f32),
            vmem((kv_heads, keys, HD), bf16),
            vmem((kv_heads, keys, 2 * HD), bf16),
            vmem((block, block), f32),
            vmem((total, columns), bf16),
            vmem((2, total, HD), f32),
            vmem((n, rows, columns), bf16),
            vmem((n, 2, rows, HD), f32),
            dma((6,)),
            dma((n,)), dma((n,)), dma((n,)), dma((n,)),
            dma((kv_heads, n)), dma((kv_heads, n)),
            dma((n,)), dma((n,)),
        ],
        compiler_params=pltpu.CompilerParams(
            collective_id=0, has_side_effects=True, vmem_limit_bytes=56 * 1024 * 1024
        ),
    )(query_pos, cache_len, q_block, kv_block, anchor_kv, cache_kv, query_q, query_kv)
    return block_out, query_out[:own]


def solution(mesh):
    in_specs = (
        P(("groups", "ctx"), "head"),
        P(None, ("groups", "ctx"), "head"),
        P(None, ("groups", "ctx"), "head"),
        P(None, ("groups", "ctx"), "head"),
        P(("groups", "ctx")),
        P(("groups", "ctx"), "head"),
        P(None, ("groups", "ctx"), "head"),
        P("groups"),
    )
    out_specs = (P(("groups", "ctx"), "head"), P(("groups", "ctx"), "head"))
    return jax.shard_map(
        functools.partial(local, mesh.shape["ctx"]),
        mesh=mesh, in_specs=in_specs, out_specs=out_specs, check_vma=False)
```

time: 165 us -> 43 us (0.26)
  blocking collectives: 76.6 us -> 0 us
  Pallas kernels: 0 us -> 37.6 us
  matrix products: 24.5 us -> 0 us
  local copies, waits for them, and re-layouts: 26.2 us -> 3.78 us
  other arithmetic: 21.9 us -> 0 us
  between operations: 15 us -> 1.29 us
    all_gather x5 -> x0, blocking collectives: 76.6 us -> none  [the longest x2 26.9 us: combined_all(): pieces = jax.tree.map(lambda part: lax.all_gather(part, axis), value)]
    pallas_call x0 -> x1, Pallas kernels: none -> 37.6 us  [local(): pl.pallas_call(functools.partial(kernel, n, own), out_shape=(jax.ShapeDty...]
    dot_general x6 -> x0, matrix products: 24.5 us -> none  [the longest x3 12.6 us: partial_attention(): jnp.einsum('rkgs,skd->rkgd', weights.astype(jnp.bfloat16), value_heads, p...]
    reduce_sum x3 -> x0, other arithmetic: 17.5 us -> none  [partial_attention(): totals = jnp.sum(weights, axis=-1)]
    slice x11 -> x0, local copies, waits for them, and re-layouts: 7.19 us -> none  [the longest x1 4.43 us: local(): cache_kv[1]]
    concatenate x10 -> x0, local copies, waits for them, and re-layouts: 5.48 us -> none  [the longest x1 2.53 us: local(): jnp.concatenate([cache_kv[0], kv_block[0]], axis=0)]
    unnamed x25 -> x2, local copies, waits for them, and re-layouts: 6.36 us -> 3.78 us
    convert_element_type x2 -> x0, other arithmetic: 2.58 us -> none  [the longest x1 1.78 us: local(): block_out = (block_parts[2] / widen(block_parts[1])).astype(jnp.bfloat16)]
  transfers between devices with their start and end apart: 1 -> 0, of which waited for: 0 -> 0; matrix products, arithmetic and copies ran while one was open for 18% -> 0% of each run, Pallas kernels for 0% -> 0%
where the time goes in v1:
time: 43 us; the launch traced here: 42.7 us
  Pallas kernels  37.6 us (87%)
  local copies, waits for them, and re-layouts  3.78 us (9%)
  between operations  1.29 us (3%)
    pallas_call x1, Pallas kernels, local(): pl.pallas_call(functools.partial(kernel, n, own), out_shape=(jax.ShapeDty...  37.6 us
    unnamed x2, local copies, waits for them, and re-layouts  3.78 us

profile of v1, /device:TPU:0, one launch (start us, length us, event | category | flops | bytes accessed | tf_op | source)
XLA Modules:
  0.0 42.7 jit_solution(267040842906343480)
XLA Ops:
  1.3 37.6 %shard_map.95 = (bf16[256,2048]{1,0:T(8,128)(2,1)}, bf16[16,2048]{1,0:T(8,128)(2,1)}) custom-call(s32[64]{0:T(128)} %pos_ref.1, s32[1]{0:T(128)S(6)} %copy.12.len_ref, bf16[256,2048]{1,0:T(8,128)(2,1)} %q_hbm.1, bf16[2,256,256]{2,1,0:T(8,128)(2,1)} %kv_hbm.1, bf16[2,128,256]{2,1,0:T(8,128)(2,1)} %anchor_hbm.1, bf16[2,4096,256]{2,1,0:T(8,128)(2,1)} %cache_hbm.1, ...), custom_call_target="tpu_custom_call" | custom-call | tf_op jit(solution)/shard_map/pallas_call | solution.py:261
  38.9 2.3 %copy.13 = bf16[256,2048]{1,0:T(8,128)(2,1)} copy(bf16[256,2048]{1,0:T(8,128)(2,1)} %get-tuple-element.4) | data formatting | bytes 2097152
  41.2 1.5 %copy.14 = bf16[16,2048]{1,0:T(8,128)(2,1)} copy(bf16[16,2048]{1,0:T(8,128)(2,1)} %get-tuple-element.5) | data formatting | bytes 131072

commit v2 on v1

v2 whole, which is shorter than its diff:
```python
import functools
import math

import jax
import jax.numpy as jnp
from jax import lax
from jax.experimental import pallas as pl
from jax.experimental.pallas import tpu as pltpu
from jax.sharding import PartitionSpec as P

HD = 128
NEG = -1e30
SCALE2 = math.log2(math.e) / math.sqrt(HD)
CHUNK = 1024
TRIM = 256
MESH = pl.DeviceIdType.MESH


def scores(queries, keys):
    dims = (((1,), (1,)), ((), ()))
    return lax.dot_general(queries, keys, dims, preferred_element_type=jnp.float32) * SCALE2


def with_ones(values):
    return jnp.concatenate([values, jnp.ones_like(values)], axis=1)


def weighted(weights, values):
    return jnp.dot(weights.astype(jnp.bfloat16), values, preferred_element_type=jnp.float32)


def kernel(
    n, own,
    pos_ref, len_hbm, q_hbm, kv_hbm, anchor_hbm, cache_hbm, qq_hbm, qkv_hbm,
    out_hbm, qout_ref,
    len_ref, q_buf, kv_buf, cache_buf, qkv_buf, anchors, queries,
    qg, kx, vx, ones, xbias, s_buf, m_run, acc, kb, vb, causal, m_blk, o_blk, out_buf,
    send_o, send_st, recv_o, recv_st,
    in_sem, out_sem, q_send, q_recv, a_send, a_recv, o_send, o_recv, st_send, st_recv,
):
    me = lax.axis_index("ctx")
    peers = [lax.rem(me + k, n) for k in range(1, n)]
    rows = qq_hbm.shape[0]
    block = q_buf.shape[0]
    columns = q_buf.shape[1]
    kv_heads = kv_buf.shape[2] // HD
    group = columns // HD // kv_heads
    share = anchor_hbm.shape[1]
    cache_count = cache_buf.shape[1]
    total = n * rows
    extra = kx.shape[1]
    tile = s_buf.shape[0]
    tile_heads = tile // total
    half = group * HD
    near_keys = block + share

    def rows_of(who):
        return pl.ds(pl.multiple_of(who * rows, rows), rows)

    def half_of(g):
        return pl.ds(g * half, half)

    loads = [
        pltpu.make_async_copy(qq_hbm, queries.at[rows_of(me)], in_sem.at[0]),
        pltpu.make_async_copy(anchor_hbm, anchors.at[me], in_sem.at[1]),
        pltpu.make_async_copy(kv_hbm, kv_buf, in_sem.at[2]),
        pltpu.make_async_copy(qkv_hbm, qkv_buf, in_sem.at[3]),
        pltpu.make_async_copy(q_hbm, q_buf, in_sem.at[4]),
        pltpu.make_async_copy(len_hbm, len_ref, in_sem.at[5]),
    ]
    cache_load = pltpu.make_async_copy(cache_hbm, cache_buf, in_sem.at[6])
    for load in loads:
        load.start()
    cache_load.start()

    barrier = pltpu.get_barrier_semaphore()
    for peer in peers:
        pl.semaphore_signal(barrier, inc=1, device_id={"ctx": peer}, device_id_type=MESH)
    pl.semaphore_wait(barrier, n - 1)

    def query_copy(g, slot, peer):
        return pltpu.make_async_remote_copy(
            src_ref=qq_hbm.at[:, half_of(g)], dst_ref=queries.at[rows_of(slot), half_of(g)],
            send_sem=q_send.at[g, peer], recv_sem=q_recv.at[g, slot],
            device_id={"ctx": peer}, device_id_type=MESH)

    def anchor_copy(slot, peer):
        return pltpu.make_async_remote_copy(
            src_ref=anchor_hbm, dst_ref=anchors.at[slot], send_sem=a_send.at[peer],
            recv_sem=a_recv.at[slot], device_id={"ctx": peer}, device_id_type=MESH)

    def output_copy(g, slot, peer):
        return pltpu.make_async_remote_copy(
            src_ref=send_o.at[rows_of(peer), half_of(g)],
            dst_ref=recv_o.at[slot, :, half_of(g)], send_sem=o_send.at[g, peer],
            recv_sem=o_recv.at[g, slot], device_id={"ctx": peer}, device_id_type=MESH)

    def stats_copy(slot, peer):
        return pltpu.make_async_remote_copy(
            src_ref=send_st.at[:, rows_of(peer)],
            dst_ref=recv_st.at[slot], send_sem=st_send.at[peer],
            recv_sem=st_recv.at[slot], device_id={"ctx": peer}, device_id_type=MESH)

    for g in range(kv_heads):
        for peer in peers:
            query_copy(g, me, peer).start()

    row = lax.broadcasted_iota(jnp.int32, (total, HD), 0)
    lane = lax.broadcasted_iota(jnp.int32, (total, HD), 1)
    row_pos = jnp.zeros((total, HD), jnp.int32)
    for i in range(n * own):
        row_pos = jnp.where(row == (i // own) * rows + i % own, pos_ref[i], row_pos)
    key_pos = jnp.full((total, HD), 1 << 30, jnp.int32)
    for j in range(own):
        key_pos = jnp.where(lane == j, pos_ref[me * own + j], key_pos)
    xbias[...] = jnp.where(key_pos <= row_pos, 0.0, NEG)
    send_st[...] = jnp.zeros_like(send_st)
    first = lax.broadcasted_iota(jnp.int32, (block, block), 0)
    second = lax.broadcasted_iota(jnp.int32, (block, block), 1)
    causal[...] = jnp.where(second <= first, 0.0, NEG)

    for load in loads:
        load.wait()
    for g in range(kv_heads):
        cols = slice(g * HD, (g + 1) * HD)
        for index, target in ((0, kx), (1, vx)):
            target[g, 0:block] = kv_buf[index, :, cols]
            target[g, pl.ds(block, share)] = anchors[me, index, :, cols]
            target[g, pl.ds(near_keys, rows)] = qkv_buf[index, :, cols]
            rest = extra - near_keys - rows
            if rest:
                target[g, pl.ds(near_keys + rows, rest)] = jnp.zeros((rest, HD), jnp.bfloat16)

    def fold(block_scores):
        parts = [block_scores[:, k:k + HD] for k in range(0, block_scores.shape[1], HD)]
        return functools.reduce(jnp.maximum, parts)

    def less(block_scores, peak):
        parts = [block_scores[:, k:k + HD] - peak for k in range(0, block_scores.shape[1], HD)]
        return jnp.concatenate(parts, axis=1)

    for g in range(kv_heads):

        def near_head(j, carry):
            head = g * group + j
            span = pl.ds(pl.multiple_of(head * HD, HD), HD)
            part = scores(q_buf[:, span], kx[g, pl.ds(0, near_keys)])
            part = jnp.concatenate([part[:, :block] + causal[...], part[:, block:]], axis=1)
            peak = jnp.max(part, axis=1, keepdims=True)
            m_blk[head] = jnp.broadcast_to(peak, (block, HD))
            o_blk[head] = weighted(jnp.exp2(part - peak), with_ones(vx[g, pl.ds(0, near_keys)]))
            return carry

        lax.fori_loop(0, group, near_head, 0, unroll=4)

    for peer in peers:
        anchor_copy(me, peer).start()

    length = len_ref[0]
    cache_load.wait()
    spare = kv_buf[0, 0:16, :][0:1]
    wide = cache_buf.shape[2]

    def trim(i, carry):
        at = pl.multiple_of(i * TRIM, TRIM)
        slot = lax.broadcasted_iota(jnp.int32, (TRIM, wide), 0) + at
        visible = jnp.where(slot < length, 1.0, 0.0).astype(jnp.bfloat16)
        keys = cache_buf[0, pl.ds(at, TRIM)]
        cache_buf[0, pl.ds(at, TRIM)] = keys * visible + spare * (1.0 - visible)
        cache_buf[1, pl.ds(at, TRIM)] = cache_buf[1, pl.ds(at, TRIM)] * visible
        ones[pl.ds(at, TRIM)] = visible[:, :HD]
        return carry

    lax.fori_loop(0, cache_count // TRIM, trim, 0)

    for g in range(kv_heads):
        cols = slice(g * HD, (g + 1) * HD)
        for peer in peers:
            query_copy(g, peer, peer).wait_recv()

        def one_tile(t, carry):
            for j in range(tile_heads):
                head = g * group + t * tile_heads + j
                qg[j * total:(j + 1) * total] = queries[:, pl.ds(pl.multiple_of(head * HD, HD), HD)]
            near = scores(qg[...], kx[g])
            tail = jnp.concatenate([xbias[...]] * tile_heads, axis=0)
            near_parts = [near[:, :near_keys], near[:, near_keys:near_keys + HD] + tail]
            if extra > near_keys + HD:
                near_parts.append(jnp.full((tile, extra - near_keys - HD), NEG, jnp.float32))
            near = jnp.concatenate(near_parts, axis=1)
            s_buf[:, cache_count:] = near
            m_run[...] = fold(near)

            def cached_scores(i, carry):
                at = pl.multiple_of(i * CHUNK, CHUNK)
                part = scores(qg[...], cache_buf[0, pl.ds(at, CHUNK), cols])
                s_buf[:, pl.ds(at, CHUNK)] = part
                m_run[...] = jnp.maximum(m_run[...], fold(part))
                return carry

            lax.fori_loop(0, cache_count // CHUNK, cached_scores, 0)
            peak = jnp.max(m_run[...], axis=1, keepdims=True)
            m_run[...] = jnp.broadcast_to(peak, m_run.shape)
            weights = jnp.exp2(less(s_buf[:, cache_count:], m_run[...]))
            acc[...] = weighted(weights, with_ones(vx[g]))

            def cached_values(i, carry):
                at = pl.multiple_of(i * CHUNK, CHUNK)
                weights = jnp.exp2(less(s_buf[:, pl.ds(at, CHUNK)], m_run[...]))
                values = jnp.concatenate(
                    [cache_buf[1, pl.ds(at, CHUNK), cols], ones[pl.ds(at, CHUNK)]], axis=1)
                acc[...] += weighted(weights, values)
                return carry

            lax.fori_loop(0, cache_count // CHUNK, cached_values, 0)
            for j in range(tile_heads):
                head = g * group + t * tile_heads + j
                span = slice(j * total, (j + 1) * total)
                send_o[:, pl.ds(pl.multiple_of(head * HD, HD), HD)] = acc[span, :HD].astype(jnp.bfloat16)
                send_st[0] = jnp.where(lane == head, m_run[span], send_st[0])
                send_st[1] = jnp.where(lane == head, acc[span, HD:], send_st[1])
            return carry

        if group == tile_heads:
            one_tile(0, 0)
        else:
            lax.fori_loop(0, group // tile_heads, one_tile, 0)
        for peer in peers:
            output_copy(g, me, peer).start()
    for peer in peers:
        stats_copy(me, peer).start()

    for peer in peers:
        anchor_copy(peer, peer).wait_recv()
    for g in range(kv_heads):
        cols = slice(g * HD, (g + 1) * HD)
        for k, peer in enumerate(peers):
            kb[g, k * share:(k + 1) * share] = anchors[peer, 0, :, cols]
            vb[g, k * share:(k + 1) * share] = with_ones(anchors[peer, 1, :, cols])

        def far_head(j, carry):
            head = g * group + j
            span = pl.ds(pl.multiple_of(head * HD, HD), HD)
            part = scores(q_buf[:, span], kb[g])
            before = m_blk[head]
            peak = jnp.maximum(before, jnp.max(part, axis=1, keepdims=True))
            result = weighted(jnp.exp2(part - peak[:, 0:1] if part.shape[1] % HD else less(part, peak)), vb[g])
            factor = jnp.exp2(before - peak)
            top = result[:, :HD] + o_blk[head, :, :HD] * factor
            below = result[:, HD:] + o_blk[head, :, HD:] * factor
            out_buf[:, span] = (top / below).astype(jnp.bfloat16)
            return carry

        lax.fori_loop(0, group, far_head, 0, unroll=4)
        pltpu.make_async_copy(out_buf.at[:, half_of(g)], out_hbm.at[:, half_of(g)], out_sem.at[g]).start()

    for peer in peers:
        stats_copy(peer, peer).wait_recv()
        for g in range(kv_heads):
            output_copy(g, peer, peer).wait_recv()
    mine = rows_of(me)
    recv_st[me] = send_st[:, mine]
    recv_o[me] = send_o[mine]
    top = functools.reduce(jnp.maximum, [recv_st[c, 0] for c in range(n)])
    factors = [jnp.exp2(recv_st[c, 0] - top) for c in range(n)]
    whole = sum(factors[c] * recv_st[c, 1] for c in range(n))
    heads = columns // HD
    for h in range(heads):
        span = slice(h * HD, (h + 1) * HD)
        merged = sum(
            recv_o[c, :, span].astype(jnp.float32) * factors[c][:, h:h + 1] for c in range(n)
        )
        qout_ref[:, span] = (merged / whole[:, h:h + 1]).astype(jnp.bfloat16)

    for g in range(kv_heads):
        pltpu.make_async_copy(out_buf.at[:, half_of(g)], out_hbm.at[:, half_of(g)], out_sem.at[g]).wait()
    for peer in peers:
        anchor_copy(me, peer).wait_send()
        stats_copy(me, peer).wait_send()
        for g in range(kv_heads):
            query_copy(g, me, peer).wait_send()
            output_copy(g, me, peer).wait_send()


def hand_on(block_in, query_in, block_out, query_out, sems):
    copies = [
        pltpu.make_async_copy(block_in, block_out, sems.at[0]),
        pltpu.make_async_copy(query_in, query_out, sems.at[1]),
    ]
    for copy in copies:
        copy.start()
    for copy in copies:
        copy.wait()


def local(n, q_block, kv_block, anchor_kv, cache_kv, cache_len, query_q, query_kv, query_pos):
    own = query_q.shape[0]
    rows = -(-own // 16) * 16
    if rows != own:
        query_q = jnp.pad(query_q, ((0, rows - own), (0, 0)))
        query_kv = jnp.pad(query_kv, ((0, 0), (0, rows - own), (0, 0)))
    block, columns = q_block.shape
    kv_columns = kv_block.shape[2]
    kv_heads = kv_columns // HD
    group = columns // kv_columns
    share = anchor_kv.shape[1]
    cache_count = cache_kv.shape[1]
    total = n * rows
    tile = total * max(1, min(group, 512 // total))
    extra = -(-(block + share + HD) // HD) * HD
    far = (n - 1) * share
    bf16, f32 = jnp.bfloat16, jnp.float32
    vmem = pltpu.VMEM
    dma = pltpu.SemaphoreType.DMA
    hbm = pl.BlockSpec(memory_space=pl.ANY)
    smem = pl.BlockSpec(memory_space=pltpu.SMEM)
    results = (
        jax.ShapeDtypeStruct((block, columns), bf16),
        jax.ShapeDtypeStruct((rows, columns), bf16),
    )
    block_out, query_out = pl.pallas_call(
        functools.partial(kernel, n, own),
        out_shape=results,
        in_specs=[smem] + [hbm] * 7,
        out_specs=(hbm, pl.BlockSpec(memory_space=vmem)),
        scratch_shapes=[
            pltpu.SMEM((1,), jnp.int32),
            vmem((block, columns), bf16),
            vmem((2, block, kv_columns), bf16),
            vmem((2, cache_count, kv_columns), bf16),
            vmem((2, rows, kv_columns), bf16),
            vmem((n, 2, share, kv_columns), bf16),
            vmem((total, columns), bf16),
            vmem((tile, HD), bf16),
            vmem((kv_heads, extra, HD), bf16),
            vmem((kv_heads, extra, HD), bf16),
            vmem((cache_count, HD), bf16),
            vmem((total, HD), f32),
            vmem((tile, cache_count + extra), f32),
            vmem((tile, HD), f32),
            vmem((tile, 2 * HD), f32),
            vmem((kv_heads, far, HD), bf16),
            vmem((kv_heads, far, 2 * HD), bf16),
            vmem((block, block), f32),
            vmem((columns // HD, block, HD), f32),
            vmem((columns // HD, block, 2 * HD), f32),
            vmem((block, columns), bf16),
            vmem((total, columns), bf16),
            vmem((2, total, HD), f32),
            vmem((n, rows, columns), bf16),
            vmem((n, 2, rows, HD), f32),
            dma((7,)), dma((kv_heads,)),
            dma((kv_heads, n)), dma((kv_heads, n)),
            dma((n,)), dma((n,)),
            dma((kv_heads, n)), dma((kv_heads, n)),
            dma((n,)), dma((n,)),
        ],
        compiler_params=pltpu.CompilerParams(
            collective_id=0, has_side_effects=True, vmem_limit_bytes=56 * 1024 * 1024
        ),
    )(query_pos, cache_len, q_block, kv_block, anchor_kv, cache_kv, query_q, query_kv)
    block_out, query_out = pl.pallas_call(
        hand_on,
        out_shape=results,
        in_specs=[hbm, hbm],
        out_specs=(hbm, hbm),
        scratch_shapes=[dma((2,))],
    )(block_out, query_out)
    return block_out, query_out[:own]


def solution(mesh):
    in_specs = (
        P(("groups", "ctx"), "head"),
        P(None, ("groups", "ctx"), "head"),
        P(None, ("groups", "ctx"), "head"),
        P(None, ("groups", "ctx"), "head"),
        P(("groups", "ctx")),
        P(("groups", "ctx"), "head"),
        P(None, ("groups", "ctx"), "head"),
        P("groups"),
    )
    out_specs = (P(("groups", "ctx"), "head"), P(("groups", "ctx"), "head"))
    return jax.shard_map(
        functools.partial(local, mesh.shape["ctx"]),
        mesh=mesh, in_specs=in_specs, out_specs=out_specs, check_vma=False)
```

time: 43 us -> 68.3 us (1.59)
  Pallas kernels: 37.6 us -> 66.9 us
  local copies, waits for them, and re-layouts: 3.78 us -> 0 us
    pallas_call x1 -> x2, Pallas kernels: 37.6 us -> 66.9 us  [the longest x1 34.9 us: local(): pl.pallas_call(hand_on, out_shape=results, in_specs=[hbm, hbm], out_specs...]
    unnamed x2 -> x0, local copies, waits for them, and re-layouts: 3.78 us -> none
where the time goes in v2:
time: 68.3 us; the launch traced here: 68.1 us
  Pallas kernels  66.9 us (98%)
  between operations  1.29 us (2%)
    pallas_call x1, Pallas kernels, local(): pl.pallas_call(hand_on, out_shape=results, in_specs=[hbm, hbm], out_specs...  34.9 us
    pallas_call x1, Pallas kernels, local(): pl.pallas_call(functools.partial(kernel, n, own), out_shape=results, in_s...  32 us

profile of v2, /device:TPU:0, one launch (start us, length us, event | category | flops | bytes accessed | tf_op | source)
XLA Modules:
  0.0 68.1 jit_solution(9527897394803703237)
XLA Ops:
  1.3 32.0 %shard_map.95 = (bf16[256,2048]{1,0:T(8,128)(2,1)}, bf16[16,2048]{1,0:T(8,128)(2,1)}) custom-call(s32[64]{0:T(128)} %pos_ref.1, s32[1]{0:T(128)S(6)} %copy.10.len_hbm, bf16[256,2048]{1,0:T(8,128)(2,1)} %q_hbm.1, bf16[2,256,256]{2,1,0:T(8,128)(2,1)} %kv_hbm.1, bf16[2,128,256]{2,1,0:T(8,128)(2,1)} %anchor_hbm.1, bf16[2,4096,256]{2,1,0:T(8,128)(2,1)} %cache_hbm.1, ...), custom_call_target="tpu_custom_call" | custom-call | tf_op jit(solution)/shard_map/pallas_call | solution.py:321
  33.3 34.9 %shard_map.96 = (bf16[256,2048]{1,0:T(8,128)(2,1)}, bf16[16,2048]{1,0:T(8,128)(2,1)}) custom-call(bf16[256,2048]{1,0:T(8,128)(2,1)} %get-tuple-element.4.block_in, bf16[16,2048]{1,0:T(8,128)(2,1)} %get-tuple-element.5.query_in), custom_call_target="tpu_custom_call" | custom-call | tf_op jit(solution)/shard_map/pallas_call | solution.py:362

commit v3 on v2

--- a/solution.py
+++ b/solution.py
@@ -13,6 +13,8 @@
 SCALE2 = math.log2(math.e) / math.sqrt(HD)
 CHUNK = 1024
 TRIM = 256
+STACK = 2
+PIECES = 4
 MESH = pl.DeviceIdType.MESH
 
 
@@ -58,7 +60,7 @@
         return pl.ds(pl.multiple_of(who * rows, rows), rows)
 
     def half_of(g):
-        return pl.ds(g * half, half)
+        return pl.ds(pl.multiple_of(g * half, half), half)
 
     loads = [
         pltpu.make_async_copy(qq_hbm, queries.at[rows_of(me)], in_sem.at[0]),
@@ -139,19 +141,24 @@
         parts = [block_scores[:, k:k + HD] - peak for k in range(0, block_scores.shape[1], HD)]
         return jnp.concatenate(parts, axis=1)
 
-    for g in range(kv_heads):
-
-        def near_head(j, carry):
-            head = g * group + j
-            span = pl.ds(pl.multiple_of(head * HD, HD), HD)
-            part = scores(q_buf[:, span], kx[g, pl.ds(0, near_keys)])
-            part = jnp.concatenate([part[:, :block] + causal[...], part[:, block:]], axis=1)
-            peak = jnp.max(part, axis=1, keepdims=True)
-            m_blk[head] = jnp.broadcast_to(peak, (block, HD))
-            o_blk[head] = weighted(jnp.exp2(part - peak), with_ones(vx[g, pl.ds(0, near_keys)]))
-            return carry
-
-        lax.fori_loop(0, group, near_head, 0, unroll=4)
+    def stacked_queries(i):
+        parts = []
+        for j in range(STACK):
+            at = pl.multiple_of((i * STACK + j) * HD, HD)
+            parts.append(q_buf[:, pl.ds(at, HD)])
+        return jnp.concatenate(parts, axis=0)
+
+    def near_heads(i, carry):
+        g = i * STACK // group
+        part = scores(stacked_queries(i), kx[g, pl.ds(0, near_keys)])
+        hidden = jnp.concatenate([causal[...]] * STACK, axis=0)
+        part = jnp.concatenate([part[:, :block] + hidden, part[:, block:]], axis=1)
+        peak = jnp.max(part, axis=1, keepdims=True)
+        m_blk[i] = jnp.broadcast_to(peak, (STACK * block, HD))
+        o_blk[i] = weighted(jnp.exp2(part - peak), with_ones(vx[g, pl.ds(0, near_keys)]))
+        return carry
+
+    lax.fori_loop(0, columns // HD // STACK, near_heads, 0)
 
     for peer in peers:
         anchor_copy(me, peer).start()
@@ -173,8 +180,8 @@
 
     lax.fori_loop(0, cache_count // TRIM, trim, 0)
 
-    for g in range(kv_heads):
-        cols = slice(g * HD, (g + 1) * HD)
+    def one_kv_head(g, carry):
+        cols = pl.ds(pl.multiple_of(g * HD, HD), HD)
         for peer in peers:
             query_copy(g, peer, peer).wait_recv()
 
@@ -227,6 +234,9 @@
             lax.fori_loop(0, group // tile_heads, one_tile, 0)
         for peer in peers:
             output_copy(g, me, peer).start()
+        return carry
+
+    lax.fori_loop(0, kv_heads, one_kv_head, 0)
     for peer in peers:
         stats_copy(me, peer).start()
 
@@ -238,20 +248,24 @@
             kb[g, k * share:(k + 1) * share] = anchors[peer, 0, :, cols]
             vb[g, k * share:(k + 1) * share] = with_ones(anchors[peer, 1, :, cols])
 
-        def far_head(j, carry):
-            head = g * group + j
-            span = pl.ds(pl.multiple_of(head * HD, HD), HD)
-            part = scores(q_buf[:, span], kb[g])
-            before = m_blk[head]
-            peak = jnp.maximum(before, jnp.max(part, axis=1, keepdims=True))
-            result = weighted(jnp.exp2(part - peak[:, 0:1] if part.shape[1] % HD else less(part, peak)), vb[g])
-            factor = jnp.exp2(before - peak)
-            top = result[:, :HD] + o_blk[head, :, :HD] * factor
-            below = result[:, HD:] + o_blk[head, :, HD:] * factor
-            out_buf[:, span] = (top / below).astype(jnp.bfloat16)
-            return carry
-
-        lax.fori_loop(0, group, far_head, 0, unroll=4)
+    def far_heads(i, carry):
+        g = i * STACK // group
+        part = scores(stacked_queries(i), kb[g])
+        before = m_blk[i]
+        peak = jnp.maximum(before, jnp.max(part, axis=1, keepdims=True))
+        result = weighted(jnp.exp2(part - peak[:, 0:1] if part.shape[1] % HD else less(part, peak)), vb[g])
+        factor = jnp.exp2(before - peak)
+        top = result[:, :HD] + o_blk[i, :, :HD] * factor
+        below = result[:, HD:] + o_blk[i, :, HD:] * factor
+        final = (top / below).astype(jnp.bfloat16)
+        for j in range(STACK):
+            at = pl.multiple_of((i * STACK + j) * HD, HD)
+            out_buf[:, pl.ds(at, HD)] = final[j * block:(j + 1) * block]
+        return carry
+
+    steps = group // STACK
+    for g in range(kv_heads):
+        lax.fori_loop(g * steps, (g + 1) * steps, far_heads, 0)
         pltpu.make_async_copy(out_buf.at[:, half_of(g)], out_hbm.at[:, half_of(g)], out_sem.at[g]).start()
 
     for peer in peers:
@@ -282,15 +296,21 @@
             output_copy(g, me, peer).wait_send()
 
 
-def hand_on(block_in, query_in, block_out, query_out, sems):
-    copies = [
-        pltpu.make_async_copy(block_in, block_out, sems.at[0]),
-        pltpu.make_async_copy(query_in, query_out, sems.at[1]),
-    ]
-    for copy in copies:
-        copy.start()
-    for copy in copies:
-        copy.wait()
+def hand_on(block_in, query_in, block_out, query_out, block_buf, query_buf, in_sems, out_sems):
+    step = block_in.shape[0] // PIECES
+    parts = [(query_in, query_buf, query_out)]
+    for k in range(PIECES):
+        span = pl.ds(k * step, step)
+        parts.append((block_in.at[span], block_buf.at[span], block_out.at[span]))
+    loads = [pltpu.make_async_copy(a, b, in_sems.at[k]) for k, (a, b, c) in enumerate(parts)]
+    stores = [pltpu.make_async_copy(b, c, out_sems.at[k]) for k, (a, b, c) in enumerate(parts)]
+    for load in loads:
+        load.start()
+    for load, store in zip(loads, stores):
+        load.wait()
+        store.start()
+    for store in stores:
+        store.wait()
 
 
 def local(n, q_block, kv_block, anchor_kv, cache_kv, cache_len, query_q, query_kv, query_pos):
@@ -342,8 +362,8 @@
             vmem((kv_heads, far, HD), bf16),
             vmem((kv_heads, far, 2 * HD), bf16),
             vmem((block, block), f32),
-            vmem((columns // HD, block, HD), f32),
-            vmem((columns // HD, block, 2 * HD), f32),
+            vmem((columns // HD // STACK, STACK * block, HD), f32),
+            vmem((columns // HD // STACK, STACK * block, 2 * HD), f32),
             vmem((block, columns), bf16),
             vmem((total, columns), bf16),
             vmem((2, total, HD), f32),
@@ -364,7 +384,9 @@
         out_shape=results,
         in_specs=[hbm, hbm],
         out_specs=(hbm, hbm),
-        scratch_shapes=[dma((2,))],
+        scratch_shapes=[
+            vmem((block, columns), bf16), vmem((rows, columns), bf16), dma((PIECES + 1,)), dma((PIECES + 1,)),
+        ],
     )(block_out, query_out)
     return block_out, query_out[:own]
 

time: 68.3 us -> 36.7 us (0.54)
  the two profiles are of different devices: /device:TPU:0 before, /device:TPU:8 now
where the time goes in v3:
time: 36.7 us; the launch traced here: 36.6 us
  Pallas kernels  35.3 us (96%)
  between operations  1.29 us (4%)
    pallas_call x1, Pallas kernels, local(): pl.pallas_call(functools.partial(kernel, n, own), out_shape=results, in_s...  33.3 us
    pallas_call x1, Pallas kernels, local(): pl.pallas_call(hand_on, out_shape=results, in_specs=[hbm, hbm], out_specs...  2.04 us

profile of v3, /device:TPU:8, one launch (start us, length us, event | category | flops | bytes accessed | tf_op | source)
XLA Modules:
  0.0 36.6 jit_solution(743673037438187720)
XLA Ops:
  1.3 33.3 %shard_map.95 = (bf16[256,2048]{1,0:T(8,128)(2,1)}, bf16[16,2048]{1,0:T(8,128)(2,1)}) custom-call(s32[64]{0:T(128)} %pos_ref.1, s32[1]{0:T(128)S(6)} %copy.10.len_hbm, bf16[256,2048]{1,0:T(8,128)(2,1)} %q_hbm.1, bf16[2,256,256]{2,1,0:T(8,128)(2,1)} %kv_hbm.1, bf16[2,128,256]{2,1,0:T(8,128)(2,1)} %anchor_hbm.1, bf16[2,4096,256]{2,1,0:T(8,128)(2,1)} %cache_hbm.1, ...), custom_call_target="tpu_custom_call" | custom-call | tf_op jit(solution)/shard_map/pallas_call | solution.py:341
  34.5 2.0 %shard_map.96 = (bf16[256,2048]{1,0:T(8,128)(2,1)}, bf16[16,2048]{1,0:T(8,128)(2,1)}) custom-call(bf16[256,2048]{1,0:T(8,128)(2,1)} %get-tuple-element.4.block_in, bf16[16,2048]{1,0:T(8,128)(2,1)} %get-tuple-element.5.query_in), custom_call_target="tpu_custom_call" | custom-call | tf_op jit(solution)/shard_map/pallas_call | solution.py:382

commit v4 on v3

--- a/solution.py
+++ b/solution.py
@@ -33,10 +33,10 @@
 
 def kernel(
     n, own,
-    pos_ref, len_hbm, q_hbm, kv_hbm, anchor_hbm, cache_hbm, qq_hbm, qkv_hbm,
+    pos_hbm, len_hbm, q_hbm, kv_hbm, anchor_hbm, cache_hbm, qq_hbm, qkv_hbm,
     out_hbm, qout_ref,
-    len_ref, q_buf, kv_buf, cache_buf, qkv_buf, anchors, queries,
-    qg, kx, vx, ones, xbias, s_buf, m_run, acc, kb, vb, causal, m_blk, o_blk, out_buf,
+    pos_ref, len_ref, q_buf, kv_buf, cache_buf, qkv_buf, anchors, queries,
+    qg, kx, vx, ones, xbias, s_bufs, m_runs, acc, kb, vb, causal, s_near, s_far, m_pair, m_blk, o_blk, out_buf,
     send_o, send_st, recv_o, recv_st,
     in_sem, out_sem, q_send, q_recv, a_send, a_recv, o_send, o_recv, st_send, st_recv,
 ):
@@ -51,7 +51,7 @@
     cache_count = cache_buf.shape[1]
     total = n * rows
     extra = kx.shape[1]
-    tile = s_buf.shape[0]
+    tile = acc.shape[0]
     tile_heads = tile // total
     half = group * HD
     near_keys = block + share
@@ -69,6 +69,7 @@
         pltpu.make_async_copy(qkv_hbm, qkv_buf, in_sem.at[3]),
         pltpu.make_async_copy(q_hbm, q_buf, in_sem.at[4]),
         pltpu.make_async_copy(len_hbm, len_ref, in_sem.at[5]),
+        pltpu.make_async_copy(pos_hbm, pos_ref, in_sem.at[7]),
     ]
     cache_load = pltpu.make_async_copy(cache_hbm, cache_buf, in_sem.at[6])
     for load in loads:
@@ -106,6 +107,9 @@
     for g in range(kv_heads):
         for peer in peers:
             query_copy(g, me, peer).start()
+
+    for load in loads:
+        load.wait()
 
     row = lax.broadcasted_iota(jnp.int32, (total, HD), 0)
     lane = lax.broadcasted_iota(jnp.int32, (total, HD), 1)
@@ -121,8 +125,6 @@
     second = lax.broadcasted_iota(jnp.int32, (block, block), 1)
     causal[...] = jnp.where(second <= first, 0.0, NEG)
 
-    for load in loads:
-        load.wait()
     for g in range(kv_heads):
         cols = slice(g * HD, (g + 1) * HD)
         for index, target in ((0, kx), (1, vx)):
@@ -138,6 +140,8 @@
         return functools.reduce(jnp.maximum, parts)
 
     def less(block_scores, peak):
+        if block_scores.shape[1] % HD:
+            return block_scores - peak[:, 0:1]
         parts = [block_scores[:, k:k + HD] - peak for k in range(0, block_scores.shape[1], HD)]
         return jnp.concatenate(parts, axis=1)
 
@@ -148,17 +152,36 @@
             parts.append(q_buf[:, pl.ds(at, HD)])
         return jnp.concatenate(parts, axis=0)
 
-    def near_heads(i, carry):
+    steps = columns // HD // STACK
+
+    def pipelined(first_step, count, begin, finish):
+        begin(first_step, 0)
+
+        def two_steps(k, carry):
+            i = first_step + 2 * k
+            begin(i + 1, 1)
+            finish(i, 0)
+            begin((i + 2) % steps, 0)
+            finish(i + 1, 1)
+            return carry
+
+        lax.fori_loop(0, count // 2, two_steps, 0)
+
+    def begin_near(i, slot):
         g = i * STACK // group
         part = scores(stacked_queries(i), kx[g, pl.ds(0, near_keys)])
         hidden = jnp.concatenate([causal[...]] * STACK, axis=0)
         part = jnp.concatenate([part[:, :block] + hidden, part[:, block:]], axis=1)
-        peak = jnp.max(part, axis=1, keepdims=True)
-        m_blk[i] = jnp.broadcast_to(peak, (STACK * block, HD))
-        o_blk[i] = weighted(jnp.exp2(part - peak), with_ones(vx[g, pl.ds(0, near_keys)]))
-        return carry
-
-    lax.fori_loop(0, columns // HD // STACK, near_heads, 0)
+        s_near[slot][...] = part
+        m_pair[slot][...] = jnp.broadcast_to(jnp.max(part, axis=1, keepdims=True), m_pair[slot].shape)
+
+    def finish_near(i, slot):
+        g = i * STACK // group
+        m_blk[i] = m_pair[slot][...]
+        weights = jnp.exp2(less(s_near[slot][...], m_pair[slot][...]))
+        o_blk[i] = weighted(weights, with_ones(vx[g, pl.ds(0, near_keys)]))
+
+    pipelined(0, steps, begin_near, finish_near)
 
     for peer in peers:
         anchor_copy(me, peer).start()
@@ -180,63 +203,79 @@
 
     lax.fori_loop(0, cache_count // TRIM, trim, 0)
 
-    def one_kv_head(g, carry):
-        cols = pl.ds(pl.multiple_of(g * HD, HD), HD)
-        for peer in peers:
-            query_copy(g, peer, peer).wait_recv()
-
-        def one_tile(t, carry):
-            for j in range(tile_heads):
-                head = g * group + t * tile_heads + j
-                qg[j * total:(j + 1) * total] = queries[:, pl.ds(pl.multiple_of(head * HD, HD), HD)]
-            near = scores(qg[...], kx[g])
-            tail = jnp.concatenate([xbias[...]] * tile_heads, axis=0)
-            near_parts = [near[:, :near_keys], near[:, near_keys:near_keys + HD] + tail]
-            if extra > near_keys + HD:
-                near_parts.append(jnp.full((tile, extra - near_keys - HD), NEG, jnp.float32))
-            near = jnp.concatenate(near_parts, axis=1)
-            s_buf[:, cache_count:] = near
-            m_run[...] = fold(near)
-
-            def cached_scores(i, carry):
-                at = pl.multiple_of(i * CHUNK, CHUNK)
-                part = scores(qg[...], cache_buf[0, pl.ds(at, CHUNK), cols])
-                s_buf[:, pl.ds(at, CHUNK)] = part
-                m_run[...] = jnp.maximum(m_run[...], fold(part))
-                return carry
-
-            lax.fori_loop(0, cache_count // CHUNK, cached_scores, 0)
-            peak = jnp.max(m_run[...], axis=1, keepdims=True)
-            m_run[...] = jnp.broadcast_to(peak, m_run.shape)
-            weights = jnp.exp2(less(s_buf[:, cache_count:], m_run[...]))
-            acc[...] = weighted(weights, with_ones(vx[g]))
-
-            def cached_values(i, carry):
-                at = pl.multiple_of(i * CHUNK, CHUNK)
-                weights = jnp.exp2(less(s_buf[:, pl.ds(at, CHUNK)], m_run[...]))
-                values = jnp.concatenate(
-                    [cache_buf[1, pl.ds(at, CHUNK), cols], ones[pl.ds(at, CHUNK)]], axis=1)
-                acc[...] += weighted(weights, values)
-                return carry
-
-            lax.fori_loop(0, cache_count // CHUNK, cached_values, 0)
-            for j in range(tile_heads):
-                head = g * group + t * tile_heads + j
-                span = slice(j * total, (j + 1) * total)
-                send_o[:, pl.ds(pl.multiple_of(head * HD, HD), HD)] = acc[span, :HD].astype(jnp.bfloat16)
-                send_st[0] = jnp.where(lane == head, m_run[span], send_st[0])
-                send_st[1] = jnp.where(lane == head, acc[span, HD:], send_st[1])
+    tiles = group // tile_heads
+    items = [(g, t) for g in range(kv_heads) for t in range(tiles)]
+
+    def open_item(k):
+        g, t = items[k]
+        s_buf, m_run, rows_in = s_bufs[k % 2], m_runs[k % 2], qg[k % 2]
+        if t == 0:
+            for peer in peers:
+                query_copy(g, peer, peer).wait_recv()
+        for j in range(tile_heads):
+            head = g * group + t * tile_heads + j
+            rows_in[j * total:(j + 1) * total] = queries[:, head * HD:(head + 1) * HD]
+        near = scores(rows_in[...], kx[g])
+        tail = jnp.concatenate([xbias[...]] * tile_heads, axis=0)
+        near_parts = [near[:, :near_keys], near[:, near_keys:near_keys + HD] + tail]
+        if extra > near_keys + HD:
+            near_parts.append(jnp.full((tile, extra - near_keys - HD), NEG, jnp.float32))
+        near = jnp.concatenate(near_parts, axis=1)
+        s_buf[:, cache_count:] = near
+        m_run[...] = fold(near)
+
+    def cached_scores(k, at):
+        g = items[k][0]
+        s_buf, m_run, rows_in = s_bufs[k % 2], m_runs[k % 2], qg[k % 2]
+        part = scores(rows_in[...], cache_buf[0, pl.ds(at, CHUNK), g * HD:(g + 1) * HD])
+        s_buf[:, pl.ds(at, CHUNK)] = part
+        m_run[...] = jnp.maximum(m_run[...], fold(part))
+
+    def near_values(k):
+        g = items[k][0]
+        s_buf, m_run = s_bufs[k % 2], m_runs[k % 2]
+        peak = jnp.max(m_run[...], axis=1, keepdims=True)
+        m_run[...] = jnp.broadcast_to(peak, m_run.shape)
+        acc[...] = weighted(jnp.exp2(less(s_buf[:, cache_count:], m_run[...])), with_ones(vx[g]))
+
+    def cached_values(k, at):
+        g = items[k][0]
+        s_buf, m_run = s_bufs[k % 2], m_runs[k % 2]
+        weights = jnp.exp2(less(s_buf[:, pl.ds(at, CHUNK)], m_run[...]))
+        values = jnp.concatenate(
+            [cache_buf[1, pl.ds(at, CHUNK), g * HD:(g + 1) * HD], ones[pl.ds(at, CHUNK)]], axis=1)
+        acc[...] += weighted(weights, values)
+
+    def close_item(k):
+        g, t = items[k]
+        m_run = m_runs[k % 2]
+        for j in range(tile_heads):
+            head = g * group + t * tile_heads + j
+            span = slice(j * total, (j + 1) * total)
+            send_o[:, head * HD:(head + 1) * HD] = acc[span, :HD].astype(jnp.bfloat16)
+            send_st[0] = jnp.where(lane == head, m_run[span], send_st[0])
+            send_st[1] = jnp.where(lane == head, acc[span, HD:], send_st[1])
+        if t == tiles - 1:
+            for peer in peers:
+                output_copy(g, me, peer).start()
+
+    for k in range(len(items) + 1):
+        if k < len(items):
+            open_item(k)
+        if k > 0:
+            near_values(k - 1)
+
+        def one_chunk(i, carry, k=k):
+            at = pl.multiple_of(i * CHUNK, CHUNK)
+            if k < len(items):
+                cached_scores(k, at)
+            if k > 0:
+                cached_values(k - 1, at)
             return carry
 
-        if group == tile_heads:
-            one_tile(0, 0)
-        else:
-            lax.fori_loop(0, group // tile_heads, one_tile, 0)
-        for peer in peers:
-            output_copy(g, me, peer).start()
-        return carry
-
-    lax.fori_loop(0, kv_heads, one_kv_head, 0)
+        lax.fori_loop(0, cache_count // CHUNK, one_chunk, 0)
+        if k > 0:
+            close_item(k - 1)
     for peer in peers:
         stats_copy(me, peer).start()
 
@@ -248,24 +287,24 @@
             kb[g, k * share:(k + 1) * share] = anchors[peer, 0, :, cols]
             vb[g, k * share:(k + 1) * share] = with_ones(anchors[peer, 1, :, cols])
 
-    def far_heads(i, carry):
-        g = i * STACK // group
-        part = scores(stacked_queries(i), kb[g])
-        before = m_blk[i]
-        peak = jnp.maximum(before, jnp.max(part, axis=1, keepdims=True))
-        result = weighted(jnp.exp2(part - peak[:, 0:1] if part.shape[1] % HD else less(part, peak)), vb[g])
-        factor = jnp.exp2(before - peak)
+    def begin_far(i, slot):
+        part = scores(stacked_queries(i), kb[i * STACK // group])
+        s_far[slot][...] = part
+        m_pair[slot][...] = jnp.maximum(m_blk[i], jnp.max(part, axis=1, keepdims=True))
+
+    def finish_far(i, slot):
+        peak = m_pair[slot][...]
+        result = weighted(jnp.exp2(less(s_far[slot][...], peak)), vb[i * STACK // group])
+        factor = jnp.exp2(m_blk[i] - peak)
         top = result[:, :HD] + o_blk[i, :, :HD] * factor
         below = result[:, HD:] + o_blk[i, :, HD:] * factor
         final = (top / below).astype(jnp.bfloat16)
         for j in range(STACK):
             at = pl.multiple_of((i * STACK + j) * HD, HD)
             out_buf[:, pl.ds(at, HD)] = final[j * block:(j + 1) * block]
-        return carry
-
-    steps = group // STACK
+
+    pipelined(0, steps, begin_far, finish_far)
     for g in range(kv_heads):
-        lax.fori_loop(g * steps, (g + 1) * steps, far_heads, 0)
         pltpu.make_async_copy(out_buf.at[:, half_of(g)], out_hbm.at[:, half_of(g)], out_sem.at[g]).start()
 
     for peer in peers:
@@ -333,7 +372,7 @@
     vmem = pltpu.VMEM
     dma = pltpu.SemaphoreType.DMA
     hbm = pl.BlockSpec(memory_space=pl.ANY)
-    smem = pl.BlockSpec(memory_space=pltpu.SMEM)
+    stacked = STACK * block
     results = (
         jax.ShapeDtypeStruct((block, columns), bf16),
         jax.ShapeDtypeStruct((rows, columns), bf16),
@@ -341,9 +380,10 @@
     block_out, query_out = pl.pallas_call(
         functools.partial(kernel, n, own),
         out_shape=results,
-        in_specs=[smem] + [hbm] * 7,
+        in_specs=[hbm] * 8,
         out_specs=(hbm, pl.BlockSpec(memory_space=vmem)),
         scratch_shapes=[
+            pltpu.SMEM(query_pos.shape, jnp.int32),
             pltpu.SMEM((1,), jnp.int32),
             vmem((block, columns), bf16),
             vmem((2, block, kv_columns), bf16),
@@ -351,17 +391,20 @@
             vmem((2, rows, kv_columns), bf16),
             vmem((n, 2, share, kv_columns), bf16),
             vmem((total, columns), bf16),
-            vmem((tile, HD), bf16),
+            [vmem((tile, HD), bf16)] * 2,
             vmem((kv_heads, extra, HD), bf16),
             vmem((kv_heads, extra, HD), bf16),
             vmem((cache_count, HD), bf16),
             vmem((total, HD), f32),
-            vmem((tile, cache_count + extra), f32),
-            vmem((tile, HD), f32),
+            [vmem((tile, cache_count + extra), f32)] * 2,
+            [vmem((tile, HD), f32)] * 2,
             vmem((tile, 2 * HD), f32),
             vmem((kv_heads, far, HD), bf16),
             vmem((kv_heads, far, 2 * HD), bf16),
             vmem((block, block), f32),
+            [vmem((stacked, block + share), f32)] * 2,
+            [vmem((stacked, far), f32)] * 2,
+            [vmem((stacked, HD), f32)] * 2,
             vmem((columns // HD // STACK, STACK * block, HD), f32),
             vmem((columns // HD // STACK, STACK * block, 2 * HD), f32),
             vmem((block, columns), bf16),
@@ -369,7 +412,7 @@
             vmem((2, total, HD), f32),
             vmem((n, rows, columns), bf16),
             vmem((n, 2, rows, HD), f32),
-            dma((7,)), dma((kv_heads,)),
+            dma((8,)), dma((kv_heads,)),
             dma((kv_heads, n)), dma((kv_heads, n)),
             dma((n,)), dma((n,)),
             dma((kv_heads, n)), dma((kv_heads, n)),

time: 36.7 us -> 34.8 us (0.948)
  the two profiles are of different devices: /device:TPU:8 before, /device:TPU:0 now
where the time goes in v4:
time: 34.8 us; the launch traced here: 34.7 us
  Pallas kernels  33.4 us (96%)
  between operations  1.29 us (4%)
    pallas_call x1, Pallas kernels, local(): pl.pallas_call(functools.partial(kernel, n, own), out_shape=results, in_s...  31.3 us
    pallas_call x1, Pallas kernels, local(): pl.pallas_call(hand_on, out_shape=results, in_specs=[hbm, hbm], out_specs...  2.04 us

profile of v4, /device:TPU:0, one launch (start us, length us, event | category | flops | bytes accessed | tf_op | source)
XLA Modules:
  0.0 34.7 jit_solution(16252937259137997214)
XLA Ops:
  1.3 31.3 %shard_map.95 = (bf16[256,2048]{1,0:T(8,128)(2,1)}, bf16[16,2048]{1,0:T(8,128)(2,1)}) custom-call(s32[64]{0:T(128)} %pos_hbm.1, s32[1]{0:T(128)S(6)} %copy.10.len_hbm, bf16[256,2048]{1,0:T(8,128)(2,1)} %q_hbm.1, bf16[2,256,256]{2,1,0:T(8,128)(2,1)} %kv_hbm.1, bf16[2,128,256]{2,1,0:T(8,128)(2,1)} %anchor_hbm.1, bf16[2,4096,256]{2,1,0:T(8,128)(2,1)} %cache_hbm.1, ...), custom_call_target="tpu_custom_call" | custom-call | tf_op jit(solution)/shard_map/pallas_call | solution.py:380
  32.6 2.0 %shard_map.96 = (bf16[256,2048]{1,0:T(8,128)(2,1)}, bf16[16,2048]{1,0:T(8,128)(2,1)}) custom-call(bf16[256,2048]{1,0:T(8,128)(2,1)} %get-tuple-element.4.block_in, bf16[16,2048]{1,0:T(8,128)(2,1)} %get-tuple-element.5.query_in), custom_call_target="tpu_custom_call" | custom-call | tf_op jit(solution)/shard_map/pallas_call | solution.py:425

commit v5 on v4

--- a/solution.py
+++ b/solution.py
@@ -54,6 +54,7 @@
     tile = acc.shape[0]
     tile_heads = tile // total
     half = group * HD
+    heads = columns // HD
     near_keys = block + share
 
     def rows_of(who):
@@ -87,10 +88,53 @@
             send_sem=q_send.at[g, peer], recv_sem=q_recv.at[g, slot],
             device_id={"ctx": peer}, device_id_type=MESH)
 
-    def anchor_copy(slot, peer):
+    ways = (1, -1)
+    reach = min(2, n - 1)
+
+    def inside(host):
+        return jnp.logical_and(host >= 0, host < n)
+
+    def anchor_direct(way, distance):
         return pltpu.make_async_remote_copy(
-            src_ref=anchor_hbm, dst_ref=anchors.at[slot], send_sem=a_send.at[peer],
-            recv_sem=a_recv.at[slot], device_id={"ctx": peer}, device_id_type=MESH)
+            src_ref=anchor_hbm, dst_ref=anchors.at[me], send_sem=a_send.at[(1 - way) // 2, distance - 1],
+            recv_sem=a_recv.at[me], device_id={"ctx": me + way * distance}, device_id_type=MESH)
+
+    def anchor_passed(way, distance):
+        origin = me - way * (distance - 1)
+        return pltpu.make_async_remote_copy(
+            src_ref=anchors.at[origin], dst_ref=anchors.at[origin],
+            send_sem=a_send.at[(1 - way) // 2, distance - 1],
+            recv_sem=a_recv.at[origin], device_id={"ctx": me + way}, device_id_type=MESH)
+
+    def for_each_direct(action):
+        for distance in range(reach, 0, -1):
+            for way in ways:
+                @pl.when(inside(me + way * distance))
+                def _():
+                    action(anchor_direct(way, distance))
+
+    def for_each_passed(action):
+        for distance in range(reach + 1, n):
+            for way in ways:
+                @pl.when(jnp.logical_and(inside(me - way * (distance - 1)), inside(me + way)))
+                def _():
+                    action(way, distance)
+
+    def pass_on(way, distance):
+        copy = anchor_passed(way, distance)
+        copy.wait_recv()
+        copy.start()
+
+    def wait_for_anchors():
+        for distance in range(1, n):
+            for way in ways:
+                here = inside(me - way * distance)
+                if reach <= distance < n - 1:
+                    here = jnp.logical_and(here, jnp.logical_not(inside(me + way)))
+
+                @pl.when(here)
+                def _():
+                    anchor_passed(way, distance + 1).wait_recv()
 
     def output_copy(g, slot, peer):
         return pltpu.make_async_remote_copy(
@@ -100,7 +144,7 @@
 
     def stats_copy(slot, peer):
         return pltpu.make_async_remote_copy(
-            src_ref=send_st.at[:, rows_of(peer)],
+            src_ref=send_st.at[rows_of(peer)],
             dst_ref=recv_st.at[slot], send_sem=st_send.at[peer],
             recv_sem=st_recv.at[slot], device_id={"ctx": peer}, device_id_type=MESH)
 
@@ -183,8 +227,7 @@
 
     pipelined(0, steps, begin_near, finish_near)
 
-    for peer in peers:
-        anchor_copy(me, peer).start()
+    for_each_direct(lambda copy: copy.start())
 
     length = len_ref[0]
     cache_load.wait()
@@ -253,8 +296,8 @@
             head = g * group + t * tile_heads + j
             span = slice(j * total, (j + 1) * total)
             send_o[:, head * HD:(head + 1) * HD] = acc[span, :HD].astype(jnp.bfloat16)
-            send_st[0] = jnp.where(lane == head, m_run[span], send_st[0])
-            send_st[1] = jnp.where(lane == head, acc[span, HD:], send_st[1])
+            marked = jnp.where(lane == head, m_run[span], send_st[...])
+            send_st[...] = jnp.where(lane == heads + head, acc[span, HD:], marked)
         if t == tiles - 1:
             for peer in peers:
                 output_copy(g, me, peer).start()
@@ -276,11 +319,12 @@
         lax.fori_loop(0, cache_count // CHUNK, one_chunk, 0)
         if k > 0:
             close_item(k - 1)
+        if k == min(1, len(items) - 1):
+            for_each_passed(pass_on)
     for peer in peers:
         stats_copy(me, peer).start()
 
-    for peer in peers:
-        anchor_copy(peer, peer).wait_recv()
+    wait_for_anchors()
     for g in range(kv_heads):
         cols = slice(g * HD, (g + 1) * HD)
         for k, peer in enumerate(peers):
@@ -312,12 +356,12 @@
         for g in range(kv_heads):
             output_copy(g, peer, peer).wait_recv()
     mine = rows_of(me)
-    recv_st[me] = send_st[:, mine]
+    recv_st[me] = send_st[mine]
     recv_o[me] = send_o[mine]
-    top = functools.reduce(jnp.maximum, [recv_st[c, 0] for c in range(n)])
-    factors = [jnp.exp2(recv_st[c, 0] - top) for c in range(n)]
-    whole = sum(factors[c] * recv_st[c, 1] for c in range(n))
-    heads = columns // HD
+    top = functools.reduce(jnp.maximum, [recv_st[c] for c in range(n)])
+    factors = [jnp.exp2(recv_st[c] - top) for c in range(n)]
+    totals = [pltpu.roll(recv_st[c], HD - heads, 1) for c in range(n)]
+    whole = sum(factors[c] * totals[c] for c in range(n))
     for h in range(heads):
         span = slice(h * HD, (h + 1) * HD)
         merged = sum(
@@ -327,8 +371,9 @@
 
     for g in range(kv_heads):
         pltpu.make_async_copy(out_buf.at[:, half_of(g)], out_hbm.at[:, half_of(g)], out_sem.at[g]).wait()
+    for_each_direct(lambda copy: copy.wait_send())
+    for_each_passed(lambda way, distance: anchor_passed(way, distance).wait_send())
     for peer in peers:
-        anchor_copy(me, peer).wait_send()
         stats_copy(me, peer).wait_send()
         for g in range(kv_heads):
             query_copy(g, me, peer).wait_send()
@@ -409,12 +454,12 @@
             vmem((columns // HD // STACK, STACK * block, 2 * HD), f32),
             vmem((block, columns), bf16),
             vmem((total, columns), bf16),
-            vmem((2, total, HD), f32),
+            vmem((total, HD), f32),
             vmem((n, rows, columns), bf16),
-            vmem((n, 2, rows, HD), f32),
+            vmem((n, rows, HD), f32),
             dma((8,)), dma((kv_heads,)),
             dma((kv_heads, n)), dma((kv_heads, n)),
-            dma((n,)), dma((n,)),
+            dma((2, n)), dma((n,)),
             dma((kv_heads, n)), dma((kv_heads, n)),
             dma((n,)), dma((n,)),
         ],

time: 34.8 us -> 32.8 us (0.943)
  Pallas kernels: 33.4 us -> 31.4 us
    pallas_call x1, Pallas kernels: 31.3 us -> 29.3 us  [local(): pl.pallas_call(functools.partial(kernel, n, own), out_shape=results, in_s...]
where the time goes in v5:
time: 32.8 us; the launch traced here: 32.7 us
  Pallas kernels  31.4 us (96%)
  between operations  1.29 us (4%)
    pallas_call x1, Pallas kernels, local(): pl.pallas_call(functools.partial(kernel, n, own), out_shape=results, in_s...  29.3 us
    pallas_call x1, Pallas kernels, local(): pl.pallas_call(hand_on, out_shape=results, in_specs=[hbm, hbm], out_specs...  2.04 us

profile of v5, /device:TPU:0, one launch (start us, length us, event | category | flops | bytes accessed | tf_op | source)
XLA Modules:
  0.0 32.7 jit_solution(16309397501563187722)
XLA Ops:
  1.3 29.3 %shard_map.95 = (bf16[256,2048]{1,0:T(8,128)(2,1)}, bf16[16,2048]{1,0:T(8,128)(2,1)}) custom-call(s32[64]{0:T(128)} %pos_hbm.1, s32[1]{0:T(128)S(6)} %copy.10.len_hbm, bf16[256,2048]{1,0:T(8,128)(2,1)} %q_hbm.1, bf16[2,256,256]{2,1,0:T(8,128)(2,1)} %kv_hbm.1, bf16[2,128,256]{2,1,0:T(8,128)(2,1)} %anchor_hbm.1, bf16[2,4096,256]{2,1,0:T(8,128)(2,1)} %cache_hbm.1, ...), custom_call_target="tpu_custom_call" | custom-call | tf_op jit(solution)/shard_map/pallas_call | solution.py:425
  30.6 2.0 %shard_map.96 = (bf16[256,2048]{1,0:T(8,128)(2,1)}, bf16[16,2048]{1,0:T(8,128)(2,1)}) custom-call(bf16[256,2048]{1,0:T(8,128)(2,1)} %get-tuple-element.4.block_in, bf16[16,2048]{1,0:T(8,128)(2,1)} %get-tuple-element.5.query_in), custom_call_target="tpu_custom_call" | custom-call | tf_op jit(solution)/shard_map/pallas_call | solution.py:470

commit v6 on v5

--- a/solution.py
+++ b/solution.py
@@ -82,50 +82,57 @@
         pl.semaphore_signal(barrier, inc=1, device_id={"ctx": peer}, device_id_type=MESH)
     pl.semaphore_wait(barrier, n - 1)
 
-    def query_copy(g, slot, peer):
-        return pltpu.make_async_remote_copy(
-            src_ref=qq_hbm.at[:, half_of(g)], dst_ref=queries.at[rows_of(slot), half_of(g)],
-            send_sem=q_send.at[g, peer], recv_sem=q_recv.at[g, slot],
-            device_id={"ctx": peer}, device_id_type=MESH)
-
     ways = (1, -1)
     reach = min(2, n - 1)
 
     def inside(host):
         return jnp.logical_and(host >= 0, host < n)
 
-    def anchor_direct(way, distance):
+    def anchor_line(slot, target, sends, direct):
         return pltpu.make_async_remote_copy(
-            src_ref=anchor_hbm, dst_ref=anchors.at[me], send_sem=a_send.at[(1 - way) // 2, distance - 1],
-            recv_sem=a_recv.at[me], device_id={"ctx": me + way * distance}, device_id_type=MESH)
-
-    def anchor_passed(way, distance):
-        origin = me - way * (distance - 1)
-        return pltpu.make_async_remote_copy(
-            src_ref=anchors.at[origin], dst_ref=anchors.at[origin],
-            send_sem=a_send.at[(1 - way) // 2, distance - 1],
-            recv_sem=a_recv.at[origin], device_id={"ctx": me + way}, device_id_type=MESH)
-
-    def for_each_direct(action):
+            src_ref=anchor_hbm if direct else anchors.at[slot], dst_ref=anchors.at[slot],
+            send_sem=a_send.at[sends], recv_sem=a_recv.at[slot],
+            device_id={"ctx": target}, device_id_type=MESH)
+
+    def query_line(g):
+        def line(slot, target, sends, direct):
+            there = queries.at[rows_of(slot), half_of(g)]
+            return pltpu.make_async_remote_copy(
+                src_ref=qq_hbm.at[:, half_of(g)] if direct else there, dst_ref=there,
+                send_sem=q_send.at[(g,) + sends], recv_sem=q_recv.at[g, slot],
+                device_id={"ctx": target}, device_id_type=MESH)
+        return line
+
+    def sender(way, distance):
+        return ((1 - way) // 2, distance - 1)
+
+    def passed(line, way, distance):
+        return line(me - way * (distance - 1), me + way, sender(way, distance), False)
+
+    def for_each_direct(line, action):
         for distance in range(reach, 0, -1):
             for way in ways:
                 @pl.when(inside(me + way * distance))
                 def _():
-                    action(anchor_direct(way, distance))
-
-    def for_each_passed(action):
+                    action(line(me, me + way * distance, sender(way, distance), True))
+
+    def for_each_passed(line, action):
         for distance in range(reach + 1, n):
             for way in ways:
                 @pl.when(jnp.logical_and(inside(me - way * (distance - 1)), inside(me + way)))
                 def _():
-                    action(way, distance)
-
-    def pass_on(way, distance):
-        copy = anchor_passed(way, distance)
-        copy.wait_recv()
-        copy.start()
-
-    def wait_for_anchors():
+                    action(passed(line, way, distance))
+
+    def begin_line(line):
+        for_each_direct(line, lambda copy: copy.start())
+
+    def pass_on(line):
+        def receive_and_send(copy):
+            copy.wait_recv()
+            copy.start()
+        for_each_passed(line, receive_and_send)
+
+    def receive(line):
         for distance in range(1, n):
             for way in ways:
                 here = inside(me - way * distance)
@@ -134,7 +141,11 @@
 
                 @pl.when(here)
                 def _():
-                    anchor_passed(way, distance + 1).wait_recv()
+                    passed(line, way, distance + 1).wait_recv()
+
+    def drain(line):
+        for_each_direct(line, lambda copy: copy.wait_send())
+        for_each_passed(line, lambda copy: copy.wait_send())
 
     def output_copy(g, slot, peer):
         return pltpu.make_async_remote_copy(
@@ -149,8 +160,7 @@
             recv_sem=st_recv.at[slot], device_id={"ctx": peer}, device_id_type=MESH)
 
     for g in range(kv_heads):
-        for peer in peers:
-            query_copy(g, me, peer).start()
+        begin_line(query_line(g))
 
     for load in loads:
         load.wait()
@@ -227,7 +237,9 @@
 
     pipelined(0, steps, begin_near, finish_near)
 
-    for_each_direct(lambda copy: copy.start())
+    for g in range(kv_heads):
+        pass_on(query_line(g))
+    begin_line(anchor_line)
 
     length = len_ref[0]
     cache_load.wait()
@@ -253,8 +265,7 @@
         g, t = items[k]
         s_buf, m_run, rows_in = s_bufs[k % 2], m_runs[k % 2], qg[k % 2]
         if t == 0:
-            for peer in peers:
-                query_copy(g, peer, peer).wait_recv()
+            receive(query_line(g))
         for j in range(tile_heads):
             head = g * group + t * tile_heads + j
             rows_in[j * total:(j + 1) * total] = queries[:, head * HD:(head + 1) * HD]
@@ -320,11 +331,11 @@
         if k > 0:
             close_item(k - 1)
         if k == min(1, len(items) - 1):
-            for_each_passed(pass_on)
+            pass_on(anchor_line)
     for peer in peers:
         stats_copy(me, peer).start()
 
-    wait_for_anchors()
+    receive(anchor_line)
     for g in range(kv_heads):
         cols = slice(g * HD, (g + 1) * HD)
         for k, peer in enumerate(peers):
@@ -371,12 +382,12 @@
 
     for g in range(kv_heads):
         pltpu.make_async_copy(out_buf.at[:, half_of(g)], out_hbm.at[:, half_of(g)], out_sem.at[g]).wait()
-    for_each_direct(lambda copy: copy.wait_send())
-    for_each_passed(lambda way, distance: anchor_passed(way, distance).wait_send())
+    drain(anchor_line)
+    for g in range(kv_heads):
+        drain(query_line(g))
     for peer in peers:
         stats_copy(me, peer).wait_send()
         for g in range(kv_heads):
-            query_copy(g, me, peer).wait_send()
             output_copy(g, me, peer).wait_send()
 
 
@@ -458,7 +469,7 @@
             vmem((n, rows, columns), bf16),
             vmem((n, rows, HD), f32),
             dma((8,)), dma((kv_heads,)),
-            dma((kv_heads, n)), dma((kv_heads, n)),
+            dma((kv_heads, 2, n)), dma((kv_heads, n)),
             dma((2, n)), dma((n,)),
             dma((kv_heads, n)), dma((kv_heads, n)),
             dma((n,)), dma((n,)),

time: 32.8 us -> 32.9 us (level)
  no operation moved by 1% of the time
where the time goes in v6:
time: 32.9 us; the launch traced here: 32.7 us
  Pallas kernels  31.4 us (95%)
  between operations  1.29 us (4%)
    pallas_call x1, Pallas kernels, local(): pl.pallas_call(functools.partial(kernel, n, own), out_shape=results, in_s...  29.4 us
    pallas_call x1, Pallas kernels, local(): pl.pallas_call(hand_on, out_shape=results, in_specs=[hbm, hbm], out_specs...  2.04 us

profile of v6, /device:TPU:0, one launch (start us, length us, event | category | flops | bytes accessed | tf_op | source)
XLA Modules:
  0.0 32.7 jit_solution(4369445112810916244)
XLA Ops:
  1.3 29.4 %shard_map.95 = (bf16[256,2048]{1,0:T(8,128)(2,1)}, bf16[16,2048]{1,0:T(8,128)(2,1)}) custom-call(s32[64]{0:T(128)} %pos_hbm.1, s32[1]{0:T(128)S(6)} %copy.10.len_hbm, bf16[256,2048]{1,0:T(8,128)(2,1)} %q_hbm.1, bf16[2,256,256]{2,1,0:T(8,128)(2,1)} %kv_hbm.1, bf16[2,128,256]{2,1,0:T(8,128)(2,1)} %anchor_hbm.1, bf16[2,4096,256]{2,1,0:T(8,128)(2,1)} %cache_hbm.1, ...), custom_call_target="tpu_custom_call" | custom-call | tf_op jit(solution)/shard_map/pallas_call | solution.py:436
  30.7 2.0 %shard_map.96 = (bf16[256,2048]{1,0:T(8,128)(2,1)}, bf16[16,2048]{1,0:T(8,128)(2,1)}) custom-call(bf16[256,2048]{1,0:T(8,128)(2,1)} %get-tuple-element.4.block_in, bf16[16,2048]{1,0:T(8,128)(2,1)} %get-tuple-element.5.query_in), custom_call_target="tpu_custom_call" | custom-call | tf_op jit(solution)/shard_map/pallas_call | solution.py:481

commit v7 on v6

--- a/solution.py
+++ b/solution.py
@@ -11,7 +11,7 @@
 HD = 128
 NEG = -1e30
 SCALE2 = math.log2(math.e) / math.sqrt(HD)
-CHUNK = 1024
+CHUNK = 2048
 TRIM = 256
 STACK = 2
 PIECES = 4
@@ -237,9 +237,6 @@
 
     pipelined(0, steps, begin_near, finish_near)
 
-    for g in range(kv_heads):
-        pass_on(query_line(g))
-    begin_line(anchor_line)
 
     length = len_ref[0]
     cache_load.wait()
@@ -257,6 +254,10 @@
         return carry
 
     lax.fori_loop(0, cache_count // TRIM, trim, 0)
+
+    for g in range(kv_heads):
+        pass_on(query_line(g))
+    begin_line(anchor_line)
 
     tiles = group // tile_heads
     items = [(g, t) for g in range(kv_heads) for t in range(tiles)]

time: 32.9 us -> 33.9 us (1.030)
  Pallas kernels: 31.4 us -> 32.5 us
    pallas_call x1, Pallas kernels: 29.4 us -> 30.4 us  [local(): pl.pallas_call(functools.partial(kernel, n, own), out_shape=results, in_s...]
where the time goes in v7:
time: 33.9 us; the launch traced here: 33.8 us
  Pallas kernels  32.5 us (96%)
  between operations  1.29 us (4%)
    pallas_call x1, Pallas kernels, local(): pl.pallas_call(functools.partial(kernel, n, own), out_shape=results, in_s...  30.4 us
    pallas_call x1, Pallas kernels, local(): pl.pallas_call(hand_on, out_shape=results, in_specs=[hbm, hbm], out_specs...  2.04 us

profile of v7, /device:TPU:0, one launch (start us, length us, event | category | flops | bytes accessed | tf_op | source)
XLA Modules:
  0.0 33.8 jit_solution(254586567978336903)
XLA Ops:
  1.3 30.4 %shard_map.95 = (bf16[256,2048]{1,0:T(8,128)(2,1)}, bf16[16,2048]{1,0:T(8,128)(2,1)}) custom-call(s32[64]{0:T(128)} %pos_hbm.1, s32[1]{0:T(128)S(6)} %copy.10.len_hbm, bf16[256,2048]{1,0:T(8,128)(2,1)} %q_hbm.1, bf16[2,256,256]{2,1,0:T(8,128)(2,1)} %kv_hbm.1, bf16[2,128,256]{2,1,0:T(8,128)(2,1)} %anchor_hbm.1, bf16[2,4096,256]{2,1,0:T(8,128)(2,1)} %cache_hbm.1, ...), custom_call_target="tpu_custom_call" | custom-call | tf_op jit(solution)/shard_map/pallas_call | solution.py:437
  31.7 2.0 %shard_map.96 = (bf16[256,2048]{1,0:T(8,128)(2,1)}, bf16[16,2048]{1,0:T(8,128)(2,1)}) custom-call(bf16[256,2048]{1,0:T(8,128)(2,1)} %get-tuple-element.4.block_in, bf16[16,2048]{1,0:T(8,128)(2,1)} %get-tuple-element.5.query_in), custom_call_target="tpu_custom_call" | custom-call | tf_op jit(solution)/shard_map/pallas_call | solution.py:482
